TPU v7x, 256 devices: a whole 4x4x8 slice. The times are simulated.
256 devices in a mesh: tm: 16 (over z_hi, y, core), dp: 16 (over z_lo, x).
Axes of the slice: x: 4, y: 4, z: 8 (z_hi: 2, z_lo: 4; z = z_hi * 4 + z_lo), core: 2. Of those that a mesh axis runs over, the one named last changes fastest.
Arguments:
- tokens: bfloat16 [16, 32, 64, 1152], P('dp', 'tm'), may hold values from -6 to 6
- clip_frames: int32 [16, 4], P('dp'), may hold values from 1 to 16, 32 in all within a row
- teacher_scores: float32 [16, 4, 8], P('dp'), may hold values from -4 to 4
- ln_gain: float32 [1152], replicated, may hold values from 0.25 to 1.75
- w_qkv: bfloat16 [1152, 3456], replicated, may hold values from -1 to 1
- w_out: bfloat16 [1152, 1152], replicated, may hold values from -0.1875 to 0.1875
- out_gain: float32 [1152], replicated, may hold values from 0.25 to 1.75
- reward_head: float32 [1152, 8], replicated, may hold values from -1.8856181 to 1.8856181
Outputs:
- scores: float32 [16, 4, 8], P('dp')
- grad_qkv: float32 [1152, 3456], P('dp')
- grad_out: float32 [1152, 1152], P('dp')
Inputs may be any that keep to these rules, and one draw needn't show every extreme that they name: `clip_frames`: each row lists the lengths of 4 clips laid end to end over its 32 frames; the longest clip of every row has exactly 16 frames.
All inputs are finite; a program needn't handle non-finite values.
Results may differ from a plain program's by a relative error of at most 0.033.
Values may be sent and summed in bfloat16 or wider, within the bound.
No kernel may reach another device: no remote copies, remote signals or barrier semaphores. Data moves between devices by JAX's collectives and lax.ppermute only.
A program may use at most 128 MiB of HBM per device.

v0:
```python
import math

import jax
import jax.numpy as jnp
from jax import lax
from jax.sharding import PartitionSpec as P

HEADS = 16
HEAD_DIM = 72
WINDOW = 8


norm_eps = 1e-06
highest = lax.Precision.HIGHEST


def passed_along(block, axis, distance):
    devices = range(lax.axis_size(axis))
    route = [(i - distance, i) for i in devices if i - distance in devices]
    return lax.ppermute(block, axis, route)


def layer_norm(values, gain_vector):
    centre = values - jnp.mean(values, axis=-1, keepdims=True)
    inv_std = lax.rsqrt(jnp.mean(centre * centre, axis=-1, keepdims=True) + norm_eps)
    normal_form = centre * inv_std
    return (normal_form * gain_vector, normal_form, inv_std)


def frame_clip(lengths, frame_ids):
    clip_ends = jnp.cumsum(lengths)
    return jnp.sum((clip_ends[None, :] <= frame_ids[:, None]).astype(jnp.int32), axis=1)


def contract_rows(left, right):
    return lax.dot_general(
        left, right, (((0,), (0,)), ((), ())), preferred_element_type=jnp.float32
    )


def on_device(tokens, clip_frames, teacher_scores, ln_gain, w_qkv, w_out, out_gain, reward_head):
    positions = tokens.shape[2]
    model_width = tokens.shape[3]
    score_scale = 1.0 / math.sqrt(HEAD_DIM)
    behind = WINDOW // 2
    key_frames = 2 + WINDOW
    frames_all = 2 * lax.axis_size("tm")
    row_count = lax.axis_size("dp")
    first_frame = 2 * lax.axis_index("tm")
    query_ids = first_frame + jnp.arange(2, dtype=jnp.int32)
    key_ids = first_frame - behind + jnp.arange(key_frames, dtype=jnp.int32)
    lengths = clip_frames[0]
    query_clip = frame_clip(lengths, query_ids)
    key_clip = frame_clip(lengths, key_ids)
    key_lag = (
        jnp.arange(key_frames, dtype=jnp.int32)[None, :] - jnp.arange(2, dtype=jnp.int32)[:, None]
    )
    allowed = (
        (key_clip[None, :] == query_clip[:, None])
        & (key_lag >= 0)
        & (key_lag < WINDOW)
        & (key_ids[None, :] >= 0)
        & (key_ids[None, :] < frames_all)
    )
    allowed_full = allowed[:, :, None, None]
    inputs = tokens[0].astype(jnp.float32)
    normed_full, _, _ = layer_norm(inputs, ln_gain)
    normed = normed_full.astype(jnp.bfloat16).reshape(2 * positions, model_width)
    projected = jnp.dot(normed, w_qkv, preferred_element_type=jnp.float32).astype(jnp.bfloat16)
    projected = projected.reshape(2, positions, 3 * model_width)
    queries = projected[:, :, :model_width]
    keyval = projected[:, :, model_width:]
    received = {}
    for offset in (2, 1, -1, -2):
        received[offset] = passed_along(keyval, "tm", offset)
    before_two, before_one, after_one, after_two = (
        received[2],
        received[1],
        received[-1],
        received[-2],
    )
    window_kv = jnp.concatenate([before_two, before_one, keyval, after_one, after_two], axis=0)
    key_window = window_kv[:, :, :model_width].reshape(key_frames, positions, HEADS, HEAD_DIM)
    value_window = window_kv[:, :, model_width:].reshape(key_frames, positions, HEADS, HEAD_DIM)
    query_heads = queries.reshape(2, positions, HEADS, HEAD_DIM)
    logits = (
        jnp.einsum("aphe,jphe->ajhp", query_heads, key_window, preferred_element_type=jnp.float32)
        * score_scale
    )
    masked = jnp.where(allowed_full, logits, -1e30)
    row_peak = jnp.max(masked, axis=1, keepdims=True)
    exp_terms = jnp.exp(masked - row_peak)
    weights = exp_terms / jnp.sum(exp_terms, axis=1, keepdims=True)
    weights_low = weights.astype(jnp.bfloat16)
    attended = jnp.einsum(
        "ajhp,jphe->aphe", weights_low, value_window, preferred_element_type=jnp.float32
    )
    attended = attended.astype(jnp.bfloat16).reshape(2 * positions, model_width)
    mixed = inputs + jnp.dot(attended, w_out, preferred_element_type=jnp.float32).reshape(
        2, positions, model_width
    )
    final_norm, centred, inv_std = layer_norm(mixed, out_gain)
    per_token = jnp.dot(
        final_norm.reshape(2 * positions, model_width), reward_head, precision=highest
    )
    frame_sums = jnp.sum(per_token.reshape(2, positions, -1), axis=1)
    onehot = (query_clip[:, None] == jnp.arange(lengths.shape[0], dtype=jnp.int32)[None, :]).astype(
        jnp.float32
    )
    clip_totals = lax.psum(jnp.dot(onehot.T, frame_sums, precision=highest), "tm")
    counts = lengths.astype(jnp.float32) * positions
    scores = clip_totals / counts[:, None]
    residue = (scores - teacher_scores[0]) / row_count
    frame_grad = jnp.dot(
        jnp.dot(onehot, residue, precision=highest), reward_head.T, precision=highest
    )
    scaled = frame_grad[:, None, :] * out_gain
    mixed_grad = (
        scaled
        - jnp.mean(scaled, axis=-1, keepdims=True)
        - centred * jnp.mean(scaled * centred, axis=-1, keepdims=True)
    ) * inv_std
    mixed_grad_low = mixed_grad.astype(jnp.bfloat16).reshape(2 * positions, model_width)
    out_part = contract_rows(attended, mixed_grad_low)
    attended_grad = lax.dot_general(
        mixed_grad_low, w_out, (((1,), (1,)), ((), ())), preferred_element_type=jnp.float32
    )
    attended_grad = attended_grad.astype(jnp.bfloat16).reshape(2, positions, HEADS, HEAD_DIM)
    weight_grad = jnp.einsum(
        "aphe,jphe->ajhp", attended_grad, value_window, preferred_element_type=jnp.float32
    )
    logit_grad = (
        weights * (weight_grad - jnp.sum(weights * weight_grad, axis=1, keepdims=True))
    ).astype(jnp.bfloat16)
    query_grad = (
        jnp.einsum("ajhp,jphe->aphe", logit_grad, key_window, preferred_element_type=jnp.float32)
        * score_scale
    )
    key_grad = (
        jnp.einsum("ajhp,aphe->jphe", logit_grad, query_heads, preferred_element_type=jnp.float32)
        * score_scale
    )
    value_grad = jnp.einsum(
        "ajhp,aphe->jphe", weights_low, attended_grad, preferred_element_type=jnp.float32
    )
    keyval_grad = jnp.concatenate(
        [
            key_grad.reshape(key_frames, positions, model_width),
            value_grad.reshape(key_frames, positions, model_width),
        ],
        axis=2,
    )
    own_rows = keyval_grad[behind : behind + 2]
    for offset, first_row in ((-2, 0), (-1, 2), (1, 6), (2, 8)):
        own_rows = own_rows + passed_along(
            keyval_grad[first_row : first_row + 2].astype(jnp.bfloat16), "tm", offset
        ).astype(jnp.float32)
    projected_grad = jnp.concatenate(
        [query_grad.reshape(2, positions, model_width), own_rows], axis=2
    )
    projected_grad = projected_grad.astype(jnp.bfloat16).reshape(2 * positions, 3 * model_width)
    qkv_part = contract_rows(normed, projected_grad)
    qkv_share, out_share = (
        lax.psum_scatter(
            qkv_part.astype(jnp.bfloat16), "dp", scatter_dimension=0, tiled=True
        ).astype(jnp.float32),
        lax.psum_scatter(
            out_part.astype(jnp.bfloat16), "dp", scatter_dimension=0, tiled=True
        ).astype(jnp.float32),
    )
    qkv_total, out_total = (
        lax.psum(qkv_share.astype(jnp.bfloat16), "tm").astype(jnp.float32),
        lax.psum(out_share.astype(jnp.bfloat16), "tm").astype(jnp.float32),
    )
    return (scores[None], qkv_total, out_total)


def solution(mesh):
    return jax.shard_map(
        on_device,
        mesh=mesh,
        in_specs=(
            P("dp", "tm", None, None),
            P("dp", None),
            P("dp", None, None),
            P(),
            P(),
            P(),
            P(),
            P(),
        ),
        out_specs=(P("dp", None, None), P("dp", None), P("dp", None)),
        check_vma=False,
    )
```

profile of v0, /device:TPU:1, one launch (start us, length us, event | category | flops | bytes accessed | tf_op | source)
XLA Modules:
  0.0 574.0 jit_solution(10888157511024265760)
XLA Ops:
  7.2 1.2 convert_reduce_fusion
  8.6 1.2 fusion.41
  10.4 1.2 fusion.38
  11.5 4.7 convolution_convert_fusion.1
  16.2 0.9 slice.40
  17.1 1.3 collective-permute-start.3
  18.4 5.1 collective-permute-start.2
  23.5 4.2 collective-permute-start.1
  27.7 2.9 collective-permute-start
  30.6 0.7 reduce-window.8
  31.3 0.8 fusion.66
  32.1 0.7 convert_reduce_fusion.1
  33.4 0.7 slice.43
  34.1 2.7 reshape.234
  37.4 10.0 %collective-permute-done = bf16[2,64,2304]{2,1,0:T(8,128)(2,1)} collective-permute-done((bf16[2,64,2304]{2,1,0:T(8,128)(2,1)}, bf16[2,64,2304]{2,1,0:T(8,128)(2,1)}, u32[]{:S(2)}, u32[]{:S(2)}) %collective-permute-start) | collective-permute-done | bytes 589856 | tf_op jit(solution)/shard_map/ppermute | solution.py:20
  47.5 1.1 constant_dynamic-update-slice_fusion.4
  48.6 1.1 constant_dynamic-update-slice_fusion.3
  49.8 1.1 constant_dynamic-update-slice_fusion.1
  50.9 1.1 constant_dynamic-update-slice_fusion
  52.0 2.0 fusion.76
  54.0 7.1 %reshape.232 = bf16[10,64,16,72]{3,2,1,0:T(8,128)(2,1)} reshape(bf16[10,64,1152]{2,1,0:T(8,128)(2,1)} %get-tuple-element.9) | data formatting | bytes 2949120 | tf_op jit(solution)/shard_map/reshape | solution.py:84
  61.1 6.8 %reshape.233 = bf16[10,64,16,72]{3,2,1,0:T(8,128)(2,1)} reshape(bf16[10,64,1152]{2,1,0:T(8,128)(2,1)} %get-tuple-element.10) | data formatting | bytes 2949120 | tf_op jit(solution)/shard_map/reshape | solution.py:83
  67.8 6.3 %fusion.7 = f32[16,64,10,2]{2,3,1,0:T(2,128)} fusion(bf16[10,64,16,72]{3,2,1,0:T(8,128)(2,1)} %reshape.233, bf16[2,64,16,72]{3,2,1,0:T(8,128)(2,1)S(1)} %copy-done.9), kind=kOutput, calls=%fused_computation.11 | convolution fusion | flops 2949120 | bytes 1851392 | tf_op jit(solution)/shard_map/aphe,jphe->ajhp/dot_general | solution.py:87
  74.2 1.5 copy.73
  76.0 1.3 copy.75
  77.3 3.9 fusion.26
  81.2 0.9 copy.76
  82.1 2.3 reshape.240
  84.4 2.3 dot_general.50
  86.6 1.7 fusion.77
  88.6 1.0 convolution_reduce_fusion
  89.6 0.8 fusion.68
  90.5 56.6 %psum.21 = f32[4,8]{1,0:T(4,128)} all-reduce(f32[4,8]{1,0:T(4,128)} %fusion.68), channel_id=1, replica_groups=mesh['tm'=16,'dp'=16] {'tm'}, use_global_device_ids=true, to_apply=%region_10.11 | all-reduce | flops 32 | bytes 256 | tf_op jit(solution)/shard_map/psum | solution.py:110
  147.1 0.9 fusion.64
  148.0 1.1 fusion.78
  149.1 0.9 multiply_reduce_fusion
  150.1 1.0 multiply_convert_fusion
  151.1 0.7 copy-done.7
  151.8 3.5 convolution_convert_fusion
  155.3 1.9 convolution_convert_fusion.2
  157.2 0.9 reshape.236
  158.2 5.4 fusion.3
  165.0 1.7 multiply_bitcast_fusion
  166.7 3.9 copy.85
  170.6 5.8 %reshape.238 = f32[10,64,1152]{2,1,0:T(8,128)} reshape(f32[10,64,16,72]{3,2,1,0:T(8,128)} %copy.85) | data formatting | bytes 5898240 | tf_op jit(solution)/shard_map/reshape | solution.py:148
  176.4 1.4 convolution_bitcast_fusion.1
  177.9 3.9 copy.88
  181.7 5.7 reshape.239
  187.5 2.2 constant_dynamic-update-slice_fusion.6
  190.8 2.2 copy-done.2
  193.0 1.4 fusion.75
  194.4 1.4 collective-permute-start.4
  195.8 4.8 collective-permute-start.7
  200.7 9.4 %collective-permute-start.6 = (bf16[2,64,2304]{2,1,0:T(8,128)(2,1)}, bf16[2,64,2304]{2,1,0:T(8,128)(2,1)}, u32[]{:S(2)}, u32[]{:S(2)}) collective-permute-start(bf16[2,64,2304]{2,1,0:T(8,128)(2,1)} %get-tuple-element.7), channel_id=1, source_target_pairs={{0,16},{16,32},{32,48},{48,64},{64,80},{80,96},{96,112},{112,128},... | collective-permute-start | bytes 1769480 | tf_op jit(solution)/shard_map/ppermute | solution.py:20
  210.1 3.5 collective-permute-start.5
  213.6 2.2 fusion.23
  216.5 5.7 collective-permute-done.6
  222.2 2.3 fusion.32
  224.5 5.5 fusion
  230.1 31.7 %reduce-scatter.11.cloned.1.call-done = bf16[72,1152]{1,0:T(8,128)(2,1)} async-done(((bf16[1152,1152]{1,0:T(8,128)(2,1)}), bf16[72,1152]{1,0:T(8,128)(2,1)}) %reduce-scatter.11.cloned.1.call-update) | async-done | bytes 165904
  261.7 118.7 %reduce-scatter.9.cloned.1.call-done = bf16[72,3456]{1,0:T(8,128)(2,1)} async-done(((bf16[1152,3456]{1,0:T(8,128)(2,1)}), bf16[72,3456]{1,0:T(8,128)(2,1)}) %reduce-scatter.9.cloned.1.call-update) | async-done | bytes 497680
  381.1 182.4 %all-reduce.5.cloned.1.call-done = (bf16[72,3456]{1,0:T(8,128)(2,1)}, bf16[72,1152]{1,0:T(8,128)(2,1)}) async-done(((bf16[72,3456]{1,0:T(8,128)(2,1)}, bf16[72,1152]{1,0:T(8,128)(2,1)}), (bf16[72,3456]{1,0:T(8,128)(2,1)}, bf16[72,1152]{1,0:T(8,128)(2,1)})) %all-reduce.5.cloned.1.call-update) | async-done | bytes 663568 | tf_op jit(solution)/shard_map/psum | solution.py:172
  563.5 1.7 convert_element_type.110
  565.2 2.0 convert_element_type.108
  (102 shorter events, 6.5 us)
Async XLA Ops:
  7.2 79.5 %copy-start = (bf16[1152,1152]{1,0:T(8,128)(2,1)S(1)}, bf16[1152,1152]{1,0:T(8,128)(2,1)}, u32[]{:S(2)}) copy-start(bf16[1152,1152]{1,0:T(8,128)(2,1)} %param.13) | copy-start | bytes 7962628
  7.2 254.6 %reduce-scatter.11.cloned.1.call-start = ((), (), s32[]{:S(2)}) async-start(), calls=%async_computation.3 | async-start | bytes 2820096
  8.5 1.4 copy-start.23
  9.8 0.6 copy-start.25
  11.5 19.0 %copy-start.31 = (s32[1,4]{1,0:T(1,128)S(1)}, s32[1,4]{1,0:T(1,128)}, u32[]{:S(2)}) copy-start(s32[1,4]{1,0:T(1,128)} %param.9) | copy-start | bytes 52
  17.1 33.8 %collective-permute-start.3 = (bf16[2,64,2304]{2,1,0:T(8,128)(2,1)}, bf16[2,64,2304]{2,1,0:T(8,128)(2,1)}, u32[]{:S(2)}, u32[]{:S(2)}) collective-permute-start(bf16[2,64,2304]{2,1,0:T(8,128)(2,1)} %slice.40), channel_id=1, source_target_pairs={{32,0},{48,16},{64,32},{80,48},{96,64},{112,80},{128,96},{144,112}... | collective-permute-start | bytes 1769480 | tf_op jit(solution)/shard_map/ppermute | solution.py:20
  18.4 31.4 %collective-permute-start.2 = (bf16[2,64,2304]{2,1,0:T(8,128)(2,1)}, bf16[2,64,2304]{2,1,0:T(8,128)(2,1)}, u32[]{:S(2)}, u32[]{:S(2)}) collective-permute-start(bf16[2,64,2304]{2,1,0:T(8,128)(2,1)} %slice.40), channel_id=1, source_target_pairs={{16,0},{32,16},{48,32},{64,48},{80,64},{96,80},{112,96},{128,112},... | collective-permute-start | bytes 1769480 | tf_op jit(solution)/shard_map/ppermute | solution.py:20
  23.5 25.0 %collective-permute-start.1 = (bf16[2,64,2304]{2,1,0:T(8,128)(2,1)}, bf16[2,64,2304]{2,1,0:T(8,128)(2,1)}, u32[]{:S(2)}, u32[]{:S(2)}) collective-permute-start(bf16[2,64,2304]{2,1,0:T(8,128)(2,1)} %slice.40), channel_id=1, source_target_pairs={{0,16},{16,32},{32,48},{48,64},{64,80},{80,96},{96,112},{112,128},... | collective-permute-start | bytes 1769480 | tf_op jit(solution)/shard_map/ppermute | solution.py:20
  27.7 19.8 %collective-permute-start = (bf16[2,64,2304]{2,1,0:T(8,128)(2,1)}, bf16[2,64,2304]{2,1,0:T(8,128)(2,1)}, u32[]{:S(2)}, u32[]{:S(2)}) collective-permute-start(bf16[2,64,2304]{2,1,0:T(8,128)(2,1)} %slice.40), channel_id=1, source_target_pairs={{0,32},{16,48},{32,64},{48,80},{64,96},{80,112},{96,128},{112,144}... | collective-permute-start | bytes 1769480 | tf_op jit(solution)/shard_map/ppermute | solution.py:20
  32.1 18.8 %copy-start.29 = (s32[2]{0:T(128)}, s32[2]{0:T(128)S(1)}, u32[]{:S(2)}) copy-start(s32[2]{0:T(128)S(1)} %fusion.66) | copy-start | bytes 28
  61.1 6.8 %copy-start.9 = (bf16[2,64,16,72]{3,2,1,0:T(8,128)(2,1)S(1)}, bf16[2,64,16,72]{3,2,1,0:T(8,128)(2,1)}, u32[]{:S(2)}) copy-start(bf16[2,64,16,72]{3,2,1,0:T(8,128)(2,1)} %reshape.234) | copy-start | bytes 884740
  67.8 7.8 %copy-start.20 = (pred[2,10]{1,0:T(4,128)(4,1)S(1)}, pred[2,10]{1,0:T(4,128)(4,1)}, u32[]{:S(2)}) copy-start(pred[2,10]{1,0:T(4,128)(4,1)} %and_and_fusion) | copy-start | bytes 64
  75.7 5.5 copy-start.5
  75.9 5.3 copy-start.14
  77.3 9.3 %copy-start.4 = (bf16[1,2,64,1152]{3,2,1,0:T(8,128)(2,1)S(1)}, bf16[1,2,64,1152]{3,2,1,0:T(8,128)(2,1)}, u32[]{:S(2)}) copy-start(bf16[1,2,64,1152]{3,2,1,0:T(8,128)(2,1)} %param.8) | copy-start | bytes 884740
  86.6 1.9 copy-start.16
  86.6 1.9 copy-start.18
  86.6 3.0 copy-start.30
  88.3 1.3 copy-start.19
  88.6 1.0 copy-start.22
  151.0 0.7 copy-start.7
  155.3 225.2 %reduce-scatter.9.cloned.1.call-start = ((), (), s32[]{:S(2)}) async-start(), calls=%async_computation.2 | async-start | bytes 8460288
  158.1 6.0 %copy-start.6 = (f32[16,64,10,2]{1,0,2,3:T(8,128)S(1)}, f32[16,64,10,2]{1,0,2,3:T(8,128)}, u32[]{:S(2)}) copy-start(f32[16,64,10,2]{1,0,2,3:T(8,128)} %copy-done.5) | copy-start | bytes 245764
  158.1 6.0 %copy-start.15 = (f32[2,16,64]{2,1,0:T(8,128)S(1)}, f32[2,16,64]{2,1,0:T(8,128)}, u32[]{:S(2)}) copy-start(f32[2,16,64]{2,1,0:T(8,128)} %copy-done.14) | copy-start | bytes 24580
  158.2 6.0 %copy-start.21 = (pred[2,10]{1,0:T(4,128)(4,1)S(1)}, pred[2,10]{1,0:T(4,128)(4,1)}, u32[]{:S(2)}) copy-start(pred[2,10]{1,0:T(4,128)(4,1)} %and_and_fusion) | copy-start | bytes 64
  163.5 1.5 copy-start.10
  165.0 1.7 copy-start.12
  170.6 5.8 %copy-start.11 = (bf16[2,10,16,64]{1,0,2,3:T(2,128)(2,1)S(1)}, bf16[2,10,16,64]{1,0,2,3:T(2,128)(2,1)}, u32[]{:S(2)}) copy-start(bf16[2,10,16,64]{1,0,2,3:T(2,128)(2,1)} %copy.75) | copy-start | bytes 122884
  187.5 2.7 copy-start.3
  190.4 2.5 copy-start.2
  193.0 20.6 %copy-start.8 = (bf16[10,64,16,72]{3,2,1,0:T(8,128)(2,1)S(1)}, bf16[10,64,16,72]{3,2,1,0:T(8,128)(2,1)}, u32[]{:S(2)}) copy-start(bf16[10,64,16,72]{3,2,1,0:T(8,128)(2,1)} %reshape.233) | copy-start | bytes 4423684
  193.0 20.6 %copy-start.13 = (bf16[2,10,16,64]{1,0,2,3:T(2,128)(2,1)S(1)}, bf16[2,10,16,64]{1,0,2,3:T(2,128)(2,1)}, u32[]{:S(2)}) copy-start(bf16[2,10,16,64]{1,0,2,3:T(2,128)(2,1)} %copy-done.12) | copy-start | bytes 122884
  194.4 22.0 %collective-permute-start.4 = (bf16[2,64,2304]{2,1,0:T(8,128)(2,1)}, bf16[2,64,2304]{2,1,0:T(8,128)(2,1)}, u32[]{:S(2)}, u32[]{:S(2)}) collective-permute-start(bf16[2,64,2304]{2,1,0:T(8,128)(2,1)} %get-tuple-element.5), channel_id=1, source_target_pairs={{32,0},{48,16},{64,32},{80,48},{96,64},{112,80},{128,96},{144,112}... | collective-permute-start | bytes 1769480 | tf_op jit(solution)/shard_map/ppermute | solution.py:20
  195.8 20.6 %collective-permute-start.7 = (bf16[2,64,2304]{2,1,0:T(8,128)(2,1)}, bf16[2,64,2304]{2,1,0:T(8,128)(2,1)}, u32[]{:S(2)}, u32[]{:S(2)}) collective-permute-start(bf16[2,64,2304]{2,1,0:T(8,128)(2,1)} %get-tuple-element.6), channel_id=1, source_target_pairs={{0,32},{16,48},{32,64},{48,80},{64,96},{80,112},{96,128},{112,144}... | collective-permute-start | bytes 1769480 | tf_op jit(solution)/shard_map/ppermute | solution.py:20
  200.7 21.5 %collective-permute-start.6 = (bf16[2,64,2304]{2,1,0:T(8,128)(2,1)}, bf16[2,64,2304]{2,1,0:T(8,128)(2,1)}, u32[]{:S(2)}, u32[]{:S(2)}) collective-permute-start(bf16[2,64,2304]{2,1,0:T(8,128)(2,1)} %get-tuple-element.7), channel_id=1, source_target_pairs={{0,16},{16,32},{32,48},{48,64},{64,80},{80,96},{96,112},{112,128},... | collective-permute-start | bytes 1769480 | tf_op jit(solution)/shard_map/ppermute | solution.py:20
  210.1 12.1 %collective-permute-start.5 = (bf16[2,64,2304]{2,1,0:T(8,128)(2,1)}, bf16[2,64,2304]{2,1,0:T(8,128)(2,1)}, u32[]{:S(2)}, u32[]{:S(2)}) collective-permute-start(bf16[2,64,2304]{2,1,0:T(8,128)(2,1)} %get-tuple-element.8), channel_id=1, source_target_pairs={{16,0},{32,16},{48,32},{64,48},{80,64},{96,80},{112,96},{128,112},... | collective-permute-start | bytes 1769480 | tf_op jit(solution)/shard_map/ppermute | solution.py:20
  215.8 8.7 %copy-start.17 = (f32[1152]{0:T(1024)S(1)}, f32[1152]{0:T(1024)}, u32[]{:S(2)}) copy-start(f32[1152]{0:T(1024)} %param.11) | copy-start | bytes 13828
  215.8 8.7 %copy-start.24 = (f32[2,64]{1,0:T(2,128)S(1)}, f32[2,64]{1,0:T(2,128)}, u32[]{:S(2)}) copy-start(f32[2,64]{1,0:T(2,128)} %copy-done.23) | copy-start | bytes 1540
  215.8 8.7 %copy-start.26 = (f32[2,64]{1,0:T(2,128)S(1)}, f32[2,64]{1,0:T(2,128)}, u32[]{:S(2)}) copy-start(f32[2,64]{1,0:T(2,128)} %copy-done.25) | copy-start | bytes 1540
  230.0 150.5 %copy-start.27 = (f32[4,8]{1,0:T(4,128)S(1)}, f32[4,8]{1,0:T(4,128)}, u32[]{:S(2)}) copy-start(f32[4,8]{1,0:T(4,128)} %psum.21) | copy-start | bytes 388
  230.0 150.5 %copy-start.28 = (f32[4]{0:T(128)S(1)}, f32[4]{0:T(128)}, u32[]{:S(2)}) copy-start(f32[4]{0:T(128)} %multiply_bitcast_fusion.1) | copy-start | bytes 52
  230.0 337.2 %copy-start.1 = (bf16[1152,1152]{1,0:T(8,128)(2,1)S(1)}, bf16[1152,1152]{1,0:T(8,128)(2,1)}, u32[]{:S(2)}) copy-start(bf16[1152,1152]{1,0:T(8,128)(2,1)} %param.13) | copy-start | bytes 7962628
  230.0 333.5 %all-reduce.5.cloned.1.call-start = ((), (), s32[]{:S(2)}) async-start(), calls=%async_computation.4 | async-start | bytes 1327104 | tf_op jit(solution)/shard_map/psum | solution.py:172
Sparse Core Ops, SparseCore 0:
  155.4 106.3 reduce-scatter.10
  264.5 115.8 reduce-scatter.8
  383.3 180.1 all-reduce.4
where the time goes:
time: 578 us; the launch traced here: 574 us
  waiting for transfers between devices  349 us (60%)
  local copies, waits for them, and re-layouts  62.8 us (11%)
  blocking collectives  56.6 us (10%)
  matrix products  41.9 us (7%)
  starting transfers between devices  32.7 us (6%)
  other arithmetic  16.8 us (3%)
  between operations  14.6 us (3%)
    psum x1, waiting for transfers between devices, on_device(): lax.psum(qkv_share.astype(jnp.bfloat16), 'tm').astype(jnp.float32)  182 us
    unnamed x5, waiting for transfers between devices  150 us
    psum x1, blocking collectives, on_device(): lax.psum(jnp.dot(onehot.T, frame_sums, precision=highest), 'tm')  56.6 us
    ppermute x8, starting transfers between devices, passed_along(): return lax.ppermute(block, axis, route)  32.6 us
    ppermute x8, waiting for transfers between devices, passed_along(): return lax.ppermute(block, axis, route)  15.7 us
  transfers between devices with their start and end apart: 11, of which 5 were waited for; matrix products, arithmetic and copies ran while one was open for 10% of the time, Pallas kernels for 0%

commit v1 on v0

v1 whole, which is shorter than its diff:
```python
import math

import jax
import jax.numpy as jnp
from jax import lax
from jax.experimental import pallas as pl
from jax.experimental.pallas import tpu as pltpu
from jax.sharding import PartitionSpec as P

HEADS = 16
HEAD_DIM = 72
WINDOW = 8
D = 1152
TOK = 128
CLIPS = 4
REWARDS = 8
ROWS = 16
CHUNK = 384
PIECE = 18
EPS = 1e-06
SCALE = 1.0 / math.sqrt(HEAD_DIM)

f32 = jnp.float32
bf16 = jnp.bfloat16
HI = lax.Precision.HIGHEST
VMEM = pl.BlockSpec(memory_space=pltpu.VMEM)
SMEM = pl.BlockSpec(memory_space=pltpu.SMEM)
ANY = pl.BlockSpec(memory_space=pl.ANY)


def dot(a, b, ca, cb, precision=None):
    return lax.dot_general(
        a, b, (((ca,), (cb,)), ((), ())), preferred_element_type=f32, precision=precision
    )


def clip_of(lens, frame):
    end, clip = lens[0], jnp.zeros_like(frame)
    for c in range(CLIPS):
        clip += (frame >= end).astype(jnp.int32)
        if c + 1 < CLIPS:
            end = end + lens[c + 1]
    return clip


def span(h):
    low = HEAD_DIM * h
    return low // 128 * 128, -(-(low + HEAD_DIM) // 128) * 128


def lane_mask(h):
    start, end = span(h)
    lane = lax.broadcasted_iota(jnp.int32, (1, end - start), 1) + (start - HEAD_DIM * h)
    return ((lane >= 0) & (lane < HEAD_DIM)).astype(f32).astype(bf16)


def standard(values):
    centre = values - jnp.mean(values, axis=-1, keepdims=True)
    inv_std = lax.rsqrt(jnp.mean(centre * centre, axis=-1, keepdims=True) + EPS)
    return centre * inv_std, inv_std


def place_rows(src, dst, pos, x_first):
    for k in range(64):
        first, second, kz = k // 16, k // 4 % 4, k % 4
        kx, ky = (first, second) if x_first else (second, first)
        dp = ((pos[2] + kz) & 3) * 4 + ((pos[0] + kx) & 3)
        start = dp * 72 + ((pos[1] + ky) & 3) * PIECE
        dst[PIECE * k : PIECE * (k + 1), :] = src[pl.ds(start, PIECE), :]


def forward_kernel(
    lens, pos, x_ref, ln_ref, wq_hbm, wo_hbm, og_ref, rh_ref,
    proj_ref, p_ref, cen_ref, inv_ref, tot_ref, keep_ref, send_ref,
    wq, wo, acc, turned, placed, sems,
):
    count = 3 * D // CHUNK
    copies = []
    for j in range(count):
        cols = pl.ds(j * CHUNK, CHUNK)
        copies.append(pltpu.make_async_copy(wq_hbm.at[:, cols], wq.at[:, cols], sems.at[j]))
    copies.append(pltpu.make_async_copy(wo_hbm, wo, sems.at[count]))
    for copy in copies:
        copy.start()
    x = x_ref[...].astype(f32)
    norm, _ = standard(x)
    normed = (norm * ln_ref[...]).astype(bf16)
    for j in range(count):
        copies[j].wait()
        cols = slice(j * CHUNK, (j + 1) * CHUNK)
        proj_ref[:, cols] = dot(normed, wq[:, cols], 1, 0).astype(bf16)
    row = lax.broadcasted_iota(jnp.int32, (TOK, TOK), 0)
    col = lax.broadcasted_iota(jnp.int32, (TOK, TOK), 1)
    lag = (col >> 2) - (row >> 2)
    allowed = (
        ((row & 3) == (col & 3))
        & (lag >= -(WINDOW // 2))
        & (lag < WINDOW - WINDOW // 2)
        & (clip_of(lens, row >> 2) == clip_of(lens, col >> 2))
    )
    acc[...] = jnp.zeros_like(acc)
    for h in range(HEADS):
        a, b = span(h)
        mask = lane_mask(h)
        logits = dot(proj_ref[:, a:b] * mask, proj_ref[:, D + a : D + b], 1, 1) * SCALE
        masked = jnp.where(allowed, logits, -1e30)
        terms = jnp.exp(masked - jnp.max(masked, axis=1, keepdims=True))
        weights = terms / jnp.sum(terms, axis=1, keepdims=True)
        p_ref[h] = weights
        acc[:, a:b] += dot(
            weights.astype(bf16), proj_ref[:, 2 * D + a : 2 * D + b] * mask, 1, 0
        )
    attended = acc[...].astype(bf16)
    copies[count].wait()
    mixed = x_ref[...].astype(f32) + dot(attended, wo[...], 1, 0)
    centred, inv_std = standard(mixed)
    cen_ref[...] = centred
    inv_ref[...] = jnp.broadcast_to(inv_std, (TOK, 128))
    final = centred * og_ref[...]
    clip_row = lax.broadcasted_iota(jnp.int32, (8, TOK), 0)
    token = lax.broadcasted_iota(jnp.int32, (8, TOK), 1)
    onehot = (clip_of(lens, token >> 2) == clip_row).astype(f32)
    tot_ref[...] = dot(dot(onehot, final, 1, 0, HI), rh_ref[...], 1, 0, HI)
    turned[0] = normed.astype(f32).T
    turned[1] = attended.astype(f32).T
    place_rows(turned.at[0], placed, pos, True)
    keep_ref[0] = placed[...].astype(bf16)
    send_ref[0] = keep_ref[0]
    which = pos[3]
    place_rows(turned.at[which], placed, pos, False)
    keep_ref[1] = placed[...].astype(bf16)
    place_rows(turned.at[1 - which], placed, pos, False)
    send_ref[1] = placed[...].astype(bf16)


def forward(lens, pos, x, ln_gain, w_qkv, w_out, out_gain, reward_head):
    shape = jax.ShapeDtypeStruct
    return pl.pallas_call(
        forward_kernel,
        out_shape=(
            shape((TOK, 3 * D), bf16),
            shape((HEADS, TOK, TOK), f32),
            shape((TOK, D), f32),
            shape((TOK, 128), f32),
            shape((8, REWARDS), f32),
            shape((2, D, TOK), bf16),
            shape((2, D, TOK), bf16),
        ),
        in_specs=[SMEM, SMEM, VMEM, VMEM, ANY, ANY, VMEM, VMEM],
        out_specs=[VMEM] * 7,
        scratch_shapes=[
            pltpu.VMEM((D, 3 * D), bf16),
            pltpu.VMEM((D, D), bf16),
            pltpu.VMEM((TOK, D), f32),
            pltpu.VMEM((2, D, TOK), f32),
            pltpu.VMEM((D, TOK), f32),
            pltpu.SemaphoreType.DMA((3 * D // CHUNK + 1,)),
        ],
        compiler_params=pltpu.CompilerParams(vmem_limit_bytes=40 << 20),
        name="forward",
    )(lens, pos, x, ln_gain, w_qkv, w_out, out_gain, reward_head)


def backward_kernel(
    lens, pos, tot_ref, teacher_ref, og_ref, rh_ref, proj_ref, p_ref, cen_ref, inv_ref, wo_ref,
    scores_ref, keep_ref, send_ref,
    dq, dk, dv, da_ref,
):
    clip_row = lax.broadcasted_iota(jnp.int32, (8, REWARDS), 0)
    count = jnp.ones((8, REWARDS), f32)
    for c in range(CLIPS):
        count = jnp.where(clip_row == c, (lens[c] * 64).astype(f32), count)
    scores = jnp.sum(tot_ref[...], axis=0) / count
    scores_ref[...] = scores
    residue = jnp.where(clip_row < CLIPS, (scores - teacher_ref[...]) / ROWS, 0.0)
    clip_grad = dot(residue, rh_ref[...], 1, 1, HI) * og_ref[...]
    token = lax.broadcasted_iota(jnp.int32, (TOK, 8), 0)
    clip = lax.broadcasted_iota(jnp.int32, (TOK, 8), 1)
    onehot = (clip_of(lens, token >> 2) == clip).astype(f32)
    scaled = dot(onehot, clip_grad, 1, 0, HI)
    centred = cen_ref[...]
    mixed_grad = (
        scaled
        - jnp.mean(scaled, axis=-1, keepdims=True)
        - centred * jnp.mean(scaled * centred, axis=-1, keepdims=True)
    ) * inv_ref[:, 0:1]
    mixed_grad = mixed_grad.astype(bf16)
    da_ref[...] = dot(mixed_grad, wo_ref[...], 1, 1).astype(bf16)
    dq[...] = jnp.zeros_like(dq)
    dk[...] = jnp.zeros_like(dk)
    dv[...] = jnp.zeros_like(dv)
    for h in range(HEADS):
        a, b = span(h)
        mask = lane_mask(h)
        out_grad = da_ref[:, a:b] * mask
        weights = p_ref[h]
        weight_grad = dot(out_grad, proj_ref[:, 2 * D + a : 2 * D + b], 1, 1)
        inner = jnp.sum(weights * weight_grad, axis=1, keepdims=True)
        logit_grad = (weights * (weight_grad - inner)).astype(bf16)
        dq[:, a:b] += dot(logit_grad, proj_ref[:, D + a : D + b] * mask, 1, 0)
        dk[:, a:b] += dot(logit_grad, proj_ref[:, a:b] * mask, 0, 0)
        dv[:, a:b] += dot(weights.astype(bf16), out_grad, 0, 0)

    def store(ref_qk, ref_vo):
        ref_qk[0] = (dq[...] * SCALE).astype(bf16)
        ref_qk[1] = (dk[...] * SCALE).astype(bf16)
        ref_vo[0] = dv[...].astype(bf16)
        ref_vo[1] = mixed_grad

    @pl.when(pos[3] == 0)
    def _():
        store(keep_ref, send_ref)

    @pl.when(pos[3] != 0)
    def _():
        store(send_ref, keep_ref)


def backward(lens, pos, totals, teacher, out_gain, reward_head, proj, p, centred, inv, w_out):
    shape = jax.ShapeDtypeStruct
    return pl.pallas_call(
        backward_kernel,
        out_shape=(
            shape((8, REWARDS), f32),
            shape((2, TOK, D), bf16),
            shape((2, TOK, D), bf16),
        ),
        in_specs=[SMEM, SMEM] + [VMEM] * 9,
        out_specs=[VMEM] * 3,
        scratch_shapes=[pltpu.VMEM((TOK, D), f32)] * 3 + [pltpu.VMEM((TOK, D), bf16)],
        compiler_params=pltpu.CompilerParams(vmem_limit_bytes=32 << 20),
        name="backward",
    )(lens, pos, totals, teacher, out_gain, reward_head, proj, p, centred, inv, w_out)


def gradient_kernel(lk, lr, rk, rr, *outs):
    for i in range(2):
        right = jnp.concatenate([rk[i], rr[i]], axis=0)
        for k in range(4):
            rows = slice(288 * k, 288 * (k + 1))
            left = jnp.concatenate([lk[i, rows], lr[i, rows]], axis=1)
            outs[4 * i + k][...] = dot(left, right, 1, 0).astype(bf16)


def gradient(left_keep, left_recv, right_keep, right_recv):
    return pl.pallas_call(
        gradient_kernel,
        out_shape=(jax.ShapeDtypeStruct((288, D), bf16),) * 8,
        in_specs=[VMEM] * 4,
        out_specs=[VMEM] * 8,
        compiler_params=pltpu.CompilerParams(vmem_limit_bytes=24 << 20),
        name="gradient",
    )(left_keep, left_recv, right_keep, right_recv)


def total(refs):
    result = refs[0][...].astype(f32)
    for ref in refs[1:]:
        result += ref[...].astype(f32)
    return result


def first_sum_kernel(*refs):
    for i in range(2):
        result = total(refs[4 * i : 4 * i + 4])
        for k in range(4):
            refs[8 + 4 * i + k][...] = result[72 * k : 72 * (k + 1)].astype(bf16)


def first_sum(parts):
    return pl.pallas_call(
        first_sum_kernel,
        out_shape=(jax.ShapeDtypeStruct((72, D), bf16),) * 8,
        in_specs=[VMEM] * 8,
        out_specs=[VMEM] * 8,
        compiler_params=pltpu.CompilerParams(vmem_limit_bytes=24 << 20),
        name="first_sum",
    )(*parts)


def second_sum_kernel(*refs):
    sums = [total(refs[0:4]), total(refs[4:8])]
    rest = jnp.zeros((6, D), f32)
    for k in range(4):
        rows = slice(PIECE * k, PIECE * (k + 1))
        refs[8 + k][...] = jnp.concatenate(
            [sums[0][rows], rest, sums[1][rows], rest], axis=0
        ).astype(bf16)


def second_sum(parts):
    return pl.pallas_call(
        second_sum_kernel,
        out_shape=(jax.ShapeDtypeStruct((48, D), bf16),) * 4,
        in_specs=[VMEM] * 8,
        out_specs=[VMEM] * 4,
        name="second_sum",
    )(*parts)


def sum_kernel(*refs):
    refs[-1][...] = total(refs[:-1]).astype(bf16)


def plain_sum(parts):
    return pl.pallas_call(
        sum_kernel,
        out_shape=jax.ShapeDtypeStruct(parts[0].shape, bf16),
        in_specs=[VMEM] * len(parts),
        out_specs=VMEM,
        name="plain_sum",
    )(*parts)


def last_kernel(pos, mine, other, qkv_ref, out_ref, held):
    for k in range(4):
        y = (pos[1] - k) & 3
        held[pos[3], y] = mine[k].astype(f32)
        held[1 - pos[3], y] = other[k].astype(f32)
    for y in range(4):
        rows = slice(PIECE * y, PIECE * (y + 1))
        qkv_ref[rows, 0:D] = held[0, y, 0:PIECE]
        qkv_ref[rows, D : 2 * D] = held[0, y, 24 : 24 + PIECE]
        qkv_ref[rows, 2 * D : 3 * D] = held[1, y, 0:PIECE]
        out_ref[rows, :] = held[1, y, 24 : 24 + PIECE]


def last(pos, mine, other):
    return pl.pallas_call(
        last_kernel,
        out_shape=(
            jax.ShapeDtypeStruct((72, 3 * D), f32),
            jax.ShapeDtypeStruct((72, D), f32),
        ),
        in_specs=[SMEM, VMEM, VMEM],
        out_specs=[VMEM] * 2,
        scratch_shapes=[pltpu.VMEM((2, 4, 48, D), f32)],
        compiler_params=pltpu.CompilerParams(vmem_limit_bytes=16 << 20),
        name="last",
    )(pos, mine, other)


def to_core(block):
    return lax.ppermute(block, "tm", [(i, i ^ 1) for i in range(16)])


def to_far(block):
    return lax.ppermute(block, "tm", [(i, i ^ 8) for i in range(16)])


def along_y(block, k):
    return lax.ppermute(block, "tm", [(i, i & 9 | (i + 2 * k) & 6) for i in range(16)])


def along_x(block, k):
    return lax.ppermute(block, "dp", [(i, i & 12 | (i + k) & 3) for i in range(16)])


def along_z(block, k):
    return lax.ppermute(block, "dp", [(i, (i + 4 * k) & 15) for i in range(16)])


def spread(move, chunks):
    moved = {k: move(chunks[k], k) for k in (1, 3, 2)}
    return [chunks[0]] + [moved[k] for k in (1, 2, 3)]


def on_device(tokens, clip_frames, teacher_scores, ln_gain, w_qkv, w_out, out_gain, reward_head):
    tm, dp = lax.axis_index("tm"), lax.axis_index("dp")
    pos = jnp.stack([dp & 3, (tm >> 1) & 3, dp >> 2, tm & 1]).astype(jnp.int32)
    lens = clip_frames[0]
    out_gain = out_gain[None]
    by_place = tokens[0].reshape(2, 16, 4, D).transpose(1, 0, 2, 3).reshape(16, 8, D)
    x = lax.all_to_all(by_place, "tm", 0, 0, tiled=True).reshape(TOK, D)
    proj, p, centred, inv, partial, left_keep, left_send = forward(
        lens, pos, x, ln_gain[None], w_qkv, w_out, out_gain, reward_head
    )
    left_recv = to_core(left_send)
    totals = lax.all_to_all(
        jnp.broadcast_to(partial, (16, 8, REWARDS)), "tm", 0, 0, tiled=True
    )
    teacher = jnp.pad(teacher_scores[0], ((0, 8 - CLIPS), (0, 0)))
    scores, right_keep, right_send = backward(
        lens, pos, totals, teacher, out_gain, reward_head, proj, p, centred, inv, w_out
    )
    parts = gradient(left_keep, left_recv, right_keep, to_core(right_send))
    a, b = spread(along_x, parts[:4]), spread(along_y, parts[4:])
    parts = first_sum(a + b)
    a, b = spread(along_y, parts[:4]), spread(along_x, parts[4:])
    part = plain_sum(spread(along_z, second_sum(a + b)))
    part = plain_sum([part, to_far(part)])
    mine = jnp.stack(spread(along_y, [part] * 4))
    qkv_total, out_total = last(pos, mine, to_core(mine))
    return (scores[None, :CLIPS], qkv_total, out_total)


def solution(mesh):
    return jax.shard_map(
        on_device,
        mesh=mesh,
        in_specs=(
            P("dp", "tm", None, None),
            P("dp", None),
            P("dp", None, None),
            P(),
            P(),
            P(),
            P(),
            P(),
        ),
        out_specs=(P("dp", None, None), P("dp", None), P("dp", None)),
        check_vma=False,
    )
```

time: 578 us -> 179 us (0.31)
  waiting for transfers between devices: 349 us -> 75.8 us
  blocking collectives: 56.6 us -> 0 us
  matrix products: 41.9 us -> 0 us
  local copies, waits for them, and re-layouts: 62.8 us -> 24.5 us
  Pallas kernels: 0 us -> 28.4 us
  other arithmetic: 16.8 us -> 1.59 us
  between operations: 14.6 us -> 0.8 us
  starting transfers between devices: 32.7 us -> 46.3 us
    psum x1 -> x0, waiting for transfers between devices: 182 us -> none  [on_device(): lax.psum(qkv_share.astype(jnp.bfloat16), 'tm').astype(jnp.float32)]
    unnamed x5 -> x0, waiting for transfers between devices: 150 us -> none
    psum x1 -> x0, blocking collectives: 56.6 us -> none  [on_device(): lax.psum(jnp.dot(onehot.T, frame_sums, precision=highest), 'tm')]
    ppermute x8 -> x22, waiting for transfers between devices: 15.7 us -> 58.5 us  [the longest x6 27.2 us: along_x(): lax.ppermute(block, 'dp', [(i, i & 12 | i + k & 3) for i in range(16)])]
    dot_general x15 -> x0, matrix products: 41.9 us -> none  [the longest x2 8.93 us: contract_rows(): lax.dot_general(left, right, (((0,), (0,)), ((), ())), preferred_element_...]
    reshape x8 -> x1, local copies, waits for them, and re-layouts: 31.7 us -> 0.79 us  [on_device(): tokens[0].reshape(2, 16, 4, D).transpose(1, 0, 2, 3).reshape(16, 8, D)]
    pallas_call x0 -> x8, Pallas kernels: none -> 28.4 us  [the longest x1 9.56 us: forward(): pl.pallas_call(forward_kernel, out_shape=(shape((TOK, 3 * D), bf16), shap...]
    all_to_all x0 -> x2, waiting for transfers between devices: none -> 17.3 us  [the longest x1 8.92 us: on_device(): lax.all_to_all(jnp.broadcast_to(partial, (16, 8, REWARDS)), 'tm', 0, 0, t...]
  transfers between devices with their start and end apart: 11 -> 24, of which waited for: 5 -> 16; matrix products, arithmetic and copies ran while one was open for 10% -> 2% of each run, Pallas kernels for 0% -> 4%
where the time goes in v1:
time: 179 us; the launch traced here: 177 us
  waiting for transfers between devices  75.8 us (42%)
  starting transfers between devices  46.3 us (26%)
  Pallas kernels  28.4 us (16%)
  local copies, waits for them, and re-layouts  24.5 us (14%)
    ppermute x6, waiting for transfers between devices, along_x(): lax.ppermute(block, 'dp', [(i, i & 12 | i + k & 3) for i in range(16)])  27.2 us
    unnamed x61, local copies, waits for them, and re-layouts  19.1 us
    ppermute x9, waiting for transfers between devices, along_y(): lax.ppermute(block, 'tm', [(i, i & 9 | i + 2 * k & 6) for i in range(16)])  15.6 us
    all_to_all x1, starting transfers between devices, on_device(): x = lax.all_to_all(by_place, 'tm', 0, 0, tiled=True).reshape(TOK, D)  12.6 us
    ppermute x9, starting transfers between devices, along_y(): lax.ppermute(block, 'tm', [(i, i & 9 | i + 2 * k & 6) for i in range(16)])  11.4 us
    pallas_call x1, Pallas kernels, forward(): pl.pallas_call(forward_kernel, out_shape=(shape((TOK, 3 * D), bf16), shap...  9.56 us
    all_to_all x1, waiting for transfers between devices, on_device(): lax.all_to_all(jnp.broadcast_to(partial, (16, 8, REWARDS)), 'tm', 0, 0, t...  8.92 us
    all_to_all x1, waiting for transfers between devices, on_device(): x = lax.all_to_all(by_place, 'tm', 0, 0, tiled=True).reshape(TOK, D)  8.41 us
  transfers between devices with their start and end apart: 24, of which 16 were waited for; matrix products, arithmetic and copies ran while one was open for 2% of the time, Pallas kernels for 4%

profile of v1, /device:TPU:1, one launch (start us, length us, event | category | flops | bytes accessed | tf_op | source)
XLA Modules:
  0.0 177.4 jit_solution(18212231348246681901)
XLA Ops:
  0.6 1.2 reshape_squeeze.3
  1.9 0.8 reshape.12
  2.7 12.6 %all-to-all-start = ((bf16[16,8,1152]{2,1,0:T(8,128)(2,1)}), bf16[16,8,1152]{2,1,0:T(8,128)(2,1)S(1)}, u32[]{:S(2)}, u32[]{:S(2)}) async-start(bf16[16,8,1152]{2,1,0:T(8,128)(2,1)} %reshape.12), calls=%async_computation | async-start | bytes 589824 | tf_op jit(solution)/shard_map/all_to_all | solution.py:374
  15.3 0.7 broadcast_in_dim.13.og_ref
  16.0 0.7 broadcast_in_dim.12.ln_ref
  16.7 1.0 copy.12.rh_ref
  17.7 0.6 pad_add_fusion.pos
  18.4 8.4 %all-to-all-done = bf16[16,8,1152]{2,1,0:T(8,128)(2,1)S(1)} async-done(((bf16[16,8,1152]{2,1,0:T(8,128)(2,1)}), bf16[16,8,1152]{2,1,0:T(8,128)(2,1)S(1)}, u32[]{:S(2)}, u32[]{:S(2)}) %all-to-all-start) | async-done | bytes 294944 | tf_op jit(solution)/shard_map/all_to_all | solution.py:374
  26.8 1.7 copy-done
  28.5 0.6 copy-done.14
  29.2 0.7 copy-done.17
  29.8 9.6 %forward.1 = (bf16[128,3456]{1,0:T(8,128)(2,1)S(1)}, f32[16,128,128]{2,1,0:T(8,128)S(1)}, f32[128,1152]{1,0:T(8,128)S(1)}, f32[128,128]{1,0:T(8,128)S(1)}, f32[8...) custom-call(s32[4]{0:T(128)S(1)} %bitcast.17, s32[4]{0:T(128)S(1)} %copy-done.14, ...), custom_call_target="tpu_custom_call" | custom-call | tf_op jit(solution)/shard_map/forward/pallas_call | solution.py:138
  39.4 1.0 copy-done.2
  40.4 0.9 copy-done.4
  41.3 0.8 copy-done.6
  42.2 0.8 copy-done.8
  43.6 0.8 copy-done.19
  44.4 0.6 broadcast_in_dim.14
  45.0 4.5 %all-to-all-start.1 = ((f32[16,8,8]{2,1,0:T(8,128)}), f32[16,8,8]{2,1,0:T(8,128)S(1)}, u32[]{:S(2)}, u32[]{:S(2)}) async-start(f32[16,8,8]{2,1,0:T(8,128)} %broadcast_in_dim.14), calls=%async_computation.1 | async-start | bytes 131072 | tf_op jit(solution)/shard_map/all_to_all | solution.py:379
  49.5 0.7 pad.4.teacher_ref
  50.3 8.9 %all-to-all-done.1.tot_ref = f32[16,8,8]{2,1,0:T(8,128)S(1)} async-done(((f32[16,8,8]{2,1,0:T(8,128)}), f32[16,8,8]{2,1,0:T(8,128)S(1)}, u32[]{:S(2)}, u32[]{:S(2)}) %all-to-all-start.1) | async-done | bytes 4128 | tf_op jit(solution)/shard_map/all_to_all | solution.py:379
  59.2 1.2 copy-done.3
  60.4 1.2 copy-done.5
  61.6 1.1 copy-done.7
  62.7 0.8 copy-done.13
  63.5 0.6 copy-done.15
  64.2 0.7 copy-done.18
  64.8 7.9 %backward.1 = (f32[8,8]{1,0:T(8,128)S(1)}, bf16[2,128,1152]{2,1,0:T(8,128)(2,1)S(1)}, bf16[2,128,1152]{2,1,0:T(8,128)(2,1)S(1)}) custom-call(s32[4]{0:T(128)S(1)} %bitcast.18, s32[4]{0:T(128)S(1)} %copy-done.15, f32[16,8,8]{2,1,0:T(8,128)S(1)} %all-to-all-done.1.tot_ref, f32[8,8]{1,0:T(8,128)S(1)} %pad.4.teacher_ref, f32[1,1152]{1,0:T(1,128)S(1)} %broadcast_in_dim.13.og_ref, ...), custom_call_target="tpu_custom_call" | custom-call | tf_op jit(solution)/shard_map/backward/pallas_call | solution.py:221
  73.3 1.6 collective-permute-done.1.rr
  74.9 1.1 copy-done.9
  76.0 2.8 %gradient.1 = (bf16[288,1152]{1,0:T(8,128)(2,1)S(1)}, bf16[288,1152]{1,0:T(8,128)(2,1)S(1)}, bf16[288,1152]{1,0:T(8,128)(2,1)S(1)}, bf16[288,1152]{1,0:T(8,128)(...) custom-call(bf16[2,1152,128]{2,1,0:T(8,128)(2,1)S(1)} %copy-done.9, ...), custom_call_target="tpu_custom_call" | custom-call | tf_op jit(solution)/shard_map/gradient/pallas_call | solution.py:246
  78.7 1.3 collective-permute-start.2
  80.0 2.5 %collective-permute-start.3 = (bf16[288,1152]{1,0:T(8,128)(2,1)S(1)}, bf16[288,1152]{1,0:T(8,128)(2,1)S(1)}, u32[]{:S(2)}, u32[]{:S(2)}) collective-permute-start(bf16[288,1152]{1,0:T(8,128)(2,1)S(1)} %get-tuple-element.47), channel_id=1, source_target_pairs={{0,2},{1,3},{2,0},{3,1},{4,6},{5,7},{6,4},{7,5},{8,10},{9,11},{10,... | collective-permute-start | bytes 1990664 | tf_op jit(solution)/shard_map/ppermute | solution.py:356
  82.5 1.1 collective-permute-start.4
  83.9 1.9 %collective-permute-start.6 = (bf16[288,1152]{1,0:T(8,128)(2,1)S(1)}, bf16[288,1152]{1,0:T(8,128)(2,1)S(1)}, u32[]{:S(2)}, u32[]{:S(2)}) collective-permute-start(bf16[288,1152]{1,0:T(8,128)(2,1)S(1)} %get-tuple-element.51), channel_id=1, source_target_pairs={{0,64},{16,80},{32,96},{48,112},{64,0},{80,16},{96,32},{112,48},{1... | collective-permute-start | bytes 1990664 | tf_op jit(solution)/shard_map/ppermute | solution.py:352
  85.8 10.4 %collective-permute-done.2.refs_1_ = bf16[288,1152]{1,0:T(8,128)(2,1)S(1)} collective-permute-done((bf16[288,1152]{1,0:T(8,128)(2,1)S(1)}, bf16[288,1152]{1,0:T(8,128)(2,1)S(1)}, u32[]{:S(2)}, u32[]{:S(2)}) %collective-permute-start.2) | collective-permute-done | bytes 663584 | tf_op jit(solution)/shard_map/ppermute | solution.py:356
  96.2 1.0 collective-permute-start.7
  97.1 14.2 %collective-permute-done.3.refs_2_ = bf16[288,1152]{1,0:T(8,128)(2,1)S(1)} collective-permute-done((bf16[288,1152]{1,0:T(8,128)(2,1)S(1)}, bf16[288,1152]{1,0:T(8,128)(2,1)S(1)}, u32[]{:S(2)}, u32[]{:S(2)}) %collective-permute-start.3) | collective-permute-done | bytes 663584 | tf_op jit(solution)/shard_map/ppermute | solution.py:356
  111.4 2.4 %collective-permute-done.6.refs_6_ = bf16[288,1152]{1,0:T(8,128)(2,1)S(1)} collective-permute-done((bf16[288,1152]{1,0:T(8,128)(2,1)S(1)}, bf16[288,1152]{1,0:T(8,128)(2,1)S(1)}, u32[]{:S(2)}, u32[]{:S(2)}) %collective-permute-start.6) | collective-permute-done | bytes 663584 | tf_op jit(solution)/shard_map/ppermute | solution.py:352
  113.8 1.7 collective-permute-done.7.refs_7_
  115.4 0.7 first_sum.1
  116.1 0.7 copy-done.10
  116.8 0.7 copy-done.11
  117.4 1.3 collective-permute-start.8
  118.8 3.3 %collective-permute-start.9 = (bf16[72,1152]{1,0:T(8,128)(2,1)S(1)}, bf16[72,1152]{1,0:T(8,128)(2,1)S(1)}, u32[]{:S(2)}, u32[]{:S(2)}) collective-permute-start(bf16[72,1152]{1,0:T(8,128)(2,1)S(1)} %get-tuple-element.55), channel_id=1, source_target_pairs={{0,64},{16,80},{32,96},{48,112},{64,0},{80,16},{96,32},{112,48},{1... | collective-permute-start | bytes 497672 | tf_op jit(solution)/shard_map/ppermute | solution.py:352
  122.4 2.0 %collective-permute-done.8.refs_1_ = bf16[72,1152]{1,0:T(8,128)(2,1)S(1)} collective-permute-done((bf16[72,1152]{1,0:T(8,128)(2,1)S(1)}, bf16[72,1152]{1,0:T(8,128)(2,1)S(1)}, u32[]{:S(2)}, u32[]{:S(2)}) %collective-permute-start.8) | collective-permute-done | bytes 165920 | tf_op jit(solution)/shard_map/ppermute | solution.py:352
  124.8 4.6 %collective-permute-done.9.refs_2_ = bf16[72,1152]{1,0:T(8,128)(2,1)S(1)} collective-permute-done((bf16[72,1152]{1,0:T(8,128)(2,1)S(1)}, bf16[72,1152]{1,0:T(8,128)(2,1)S(1)}, u32[]{:S(2)}, u32[]{:S(2)}) %collective-permute-start.9) | collective-permute-done | bytes 165920 | tf_op jit(solution)/shard_map/ppermute | solution.py:352
  129.5 2.6 %collective-permute-done.11.refs_5_ = bf16[72,1152]{1,0:T(8,128)(2,1)S(1)} collective-permute-done((bf16[72,1152]{1,0:T(8,128)(2,1)S(1)}, bf16[72,1152]{1,0:T(8,128)(2,1)S(1)}, u32[]{:S(2)}, u32[]{:S(2)}) %collective-permute-start.11) | collective-permute-done | bytes 165920 | tf_op jit(solution)/shard_map/ppermute | solution.py:356
  132.9 2.2 %second_sum.1 = (bf16[48,1152]{1,0:T(8,128)(2,1)}, bf16[48,1152]{1,0:T(8,128)(2,1)}, bf16[48,1152]{1,0:T(8,128)(2,1)}, bf16[48,1152]{1,0:T(8,128)(2,1)}) custom-call(bf16[72,1152]{1,0:T(8,128)(2,1)} %copy-done.10, bf16[72,1152]{1,0:T(8,128)(2,1)} %copy-done.20, bf16[72,1152]{1,0:T(8,128)(2,1)} %copy-done.21, bf16[72,1152]{1,0:T(8,128)(2,1)} %copy-done.22, ...), custom_call_target="tpu_custom_call" | custom-call | tf_op jit(solution)/shard_map/second_sum/pallas_call | solution.py:292
  135.1 3.8 %collective-permute-start.14 = (bf16[48,1152]{1,0:T(8,128)(2,1)}, bf16[48,1152]{1,0:T(8,128)(2,1)S(1)}, u32[]{:S(2)}, u32[]{:S(2)}) collective-permute-start(bf16[48,1152]{1,0:T(8,128)(2,1)} %get-tuple-element.62), channel_id=1, source_target_pairs={{0,4},{1,5},{2,6},{3,7},{4,8},{5,9},{6,10},{7,11},{8,12},{9,13},{1... | collective-permute-start | bytes 331784 | tf_op jit(solution)/shard_map/ppermute | solution.py:360
  139.4 2.3 %collective-permute-start.16 = (bf16[48,1152]{1,0:T(8,128)(2,1)}, bf16[48,1152]{1,0:T(8,128)(2,1)S(1)}, u32[]{:S(2)}, u32[]{:S(2)}) collective-permute-start(bf16[48,1152]{1,0:T(8,128)(2,1)} %get-tuple-element.64), channel_id=1, source_target_pairs={{0,12},{1,13},{2,14},{3,15},{4,0},{5,1},{6,2},{7,3},{8,4},{9,5},{1... | collective-permute-start | bytes 331784 | tf_op jit(solution)/shard_map/ppermute | solution.py:360
  141.7 5.6 %collective-permute-done.15.refs_2_ = bf16[48,1152]{1,0:T(8,128)(2,1)S(1)} collective-permute-done((bf16[48,1152]{1,0:T(8,128)(2,1)}, bf16[48,1152]{1,0:T(8,128)(2,1)S(1)}, u32[]{:S(2)}, u32[]{:S(2)}) %collective-permute-start.15) | collective-permute-done | bytes 110624 | tf_op jit(solution)/shard_map/ppermute | solution.py:360
  147.3 0.6 copy-done.28
  148.0 1.7 plain_sum.2.refs_0_
  150.1 7.6 %collective-permute-done.17.refs_1_ = bf16[48,1152]{1,0:T(8,128)(2,1)S(1)} collective-permute-done((bf16[48,1152]{1,0:T(8,128)(2,1)}, bf16[48,1152]{1,0:T(8,128)(2,1)S(1)}, u32[]{:S(2)}, u32[]{:S(2)}) %collective-permute-start.17) | collective-permute-done | bytes 110624 | tf_op jit(solution)/shard_map/ppermute | solution.py:348
  157.7 0.6 copy-done.26
  158.4 1.6 plain_sum.3
  160.2 3.0 %collective-permute-start.19 = (bf16[48,1152]{1,0:T(8,128)(2,1)}, bf16[48,1152]{1,0:T(8,128)(2,1)S(1)}, u32[]{:S(2)}, u32[]{:S(2)}) collective-permute-start(bf16[48,1152]{1,0:T(8,128)(2,1)} %plain_sum.3), channel_id=1, source_target_pairs={{0,64},{16,80},{32,96},{48,112},{64,0},{80,16},{96,32},{112,48},{1... | collective-permute-start | bytes 331784 | tf_op jit(solution)/shard_map/ppermute | solution.py:352
  163.8 1.8 %collective-permute-done.19 = bf16[48,1152]{1,0:T(8,128)(2,1)S(1)} collective-permute-done((bf16[48,1152]{1,0:T(8,128)(2,1)}, bf16[48,1152]{1,0:T(8,128)(2,1)S(1)}, u32[]{:S(2)}, u32[]{:S(2)}) %collective-permute-start.19) | collective-permute-done | bytes 110624 | tf_op jit(solution)/shard_map/ppermute | solution.py:352
  165.6 2.9 %collective-permute-done.18 = bf16[48,1152]{1,0:T(8,128)(2,1)S(1)} collective-permute-done((bf16[48,1152]{1,0:T(8,128)(2,1)}, bf16[48,1152]{1,0:T(8,128)(2,1)S(1)}, u32[]{:S(2)}, u32[]{:S(2)}) %collective-permute-start.18) | collective-permute-done | bytes 110624 | tf_op jit(solution)/shard_map/ppermute | solution.py:352
  168.6 1.0 pad_maximum_fusion.mine
  169.5 4.6 %collective-permute-start.21 = (bf16[4,48,1152]{2,1,0:T(8,128)(2,1)S(1)}, bf16[4,48,1152]{2,1,0:T(8,128)(2,1)S(1)}, u32[]{:S(2)}, u32[]{:S(2)}) collective-permute-start(bf16[4,48,1152]{2,1,0:T(8,128)(2,1)S(1)} %pad_maximum_fusion.mine), channel_id=1, source_target_pairs={{0,16},{16,0},{32,48},{48,32},{64,80},{80,64},{96,112},{112,96},{1... | collective-permute-start | bytes 1327112 | tf_op jit(solution)/shard_map/ppermute | solution.py:344
  174.7 0.8 collective-permute-done.21.other
  175.5 1.9 %last.1 = (f32[72,3456]{1,0:T(8,128)}, f32[72,1152]{1,0:T(8,128)}) custom-call(s32[4]{0:T(128)S(1)} %copy-done.16, bf16[4,48,1152]{2,1,0:T(8,128)(2,1)S(1)} %pad_maximum_fusion.mine, bf16[4,48,1152]{2,1,0:T(8,128)(2,1)S(1)} %collective-permute-done.21.other), custom_call_target="tpu_custom_call" | custom-call | tf_op jit(solution)/shard_map/last/pallas_call | solution.py:329
  (63 shorter events, 5.6 us)
Async XLA Ops:
  0.6 58.6 %copy-start.1 = (bf16[1152,1152]{1,0:T(8,128)(2,1)S(1)}, bf16[1152,1152]{1,0:T(8,128)(2,1)}, u32[]{:S(2)}) copy-start(bf16[1152,1152]{1,0:T(8,128)(2,1)} %wo_ref.1) | copy-start | bytes 7962628
  2.7 24.1 %all-to-all-start = ((bf16[16,8,1152]{2,1,0:T(8,128)(2,1)}), bf16[16,8,1152]{2,1,0:T(8,128)(2,1)S(1)}, u32[]{:S(2)}, u32[]{:S(2)}) async-start(bf16[16,8,1152]{2,1,0:T(8,128)(2,1)} %reshape.12), calls=%async_computation | async-start | bytes 589824 | tf_op jit(solution)/shard_map/all_to_all | solution.py:374
  26.8 1.8 copy-start
  28.5 0.6 copy-start.14
  29.2 0.7 copy-start.17
  39.4 1.0 copy-start.2
  40.4 0.9 copy-start.4
  41.3 0.8 copy-start.6
  42.2 0.8 copy-start.8
  43.0 0.6 copy-start.12
  43.6 0.8 copy-start.19
  45.0 14.2 %all-to-all-start.1 = ((f32[16,8,8]{2,1,0:T(8,128)}), f32[16,8,8]{2,1,0:T(8,128)S(1)}, u32[]{:S(2)}, u32[]{:S(2)}) async-start(f32[16,8,8]{2,1,0:T(8,128)} %broadcast_in_dim.14), calls=%async_computation.1 | async-start | bytes 131072 | tf_op jit(solution)/shard_map/all_to_all | solution.py:379
  50.2 23.1 %collective-permute-start = (bf16[2,1152,128]{2,1,0:T(8,128)(2,1)}, bf16[2,1152,128]{2,1,0:T(8,128)(2,1)}, u32[]{:S(2)}, u32[]{:S(2)}) collective-permute-start(bf16[2,1152,128]{2,1,0:T(8,128)(2,1)} %copy-done.19), channel_id=1, source_target_pairs={{0,16},{16,0},{32,48},{48,32},{64,80},{80,64},{96,112},{112,96},{1... | collective-permute-start | bytes 1769480 | tf_op jit(solution)/shard_map/ppermute | solution.py:344
  59.2 1.2 copy-start.3
  60.4 1.2 copy-start.5
  61.6 1.1 copy-start.7
  62.7 0.8 copy-start.13
  63.5 0.6 copy-start.15
  64.2 0.7 copy-start.18
  64.8 110.7 %copy-start.16 = (s32[4]{0:T(128)S(1)}, s32[4]{0:T(128)}, u32[]{:S(2)}) copy-start(s32[4]{0:T(128)} %pad_add_fusion.pos) | copy-start | bytes 52
  72.8 2.1 %collective-permute-start.1 = (bf16[2,128,1152]{2,1,0:T(8,128)(2,1)S(1)}, bf16[2,128,1152]{2,1,0:T(8,128)(2,1)S(1)}, u32[]{:S(2)}, u32[]{:S(2)}) collective-permute-start(bf16[2,128,1152]{2,1,0:T(8,128)(2,1)S(1)} %get-tuple-element.44), channel_id=1, source_target_pairs={{0,16},{16,0},{32,48},{48,32},{64,80},{80,64},{96,112},{112,96},{1... | collective-permute-start | bytes 1769480 | tf_op jit(solution)/shard_map/ppermute | solution.py:344
  74.9 1.1 copy-start.9
  78.7 17.4 %collective-permute-start.2 = (bf16[288,1152]{1,0:T(8,128)(2,1)S(1)}, bf16[288,1152]{1,0:T(8,128)(2,1)S(1)}, u32[]{:S(2)}, u32[]{:S(2)}) collective-permute-start(bf16[288,1152]{1,0:T(8,128)(2,1)S(1)} %get-tuple-element.46), channel_id=1, source_target_pairs={{0,1},{1,2},{2,3},{3,0},{4,5},{5,6},{6,7},{7,4},{8,9},{9,10},{10,1... | collective-permute-start | bytes 1990664 | tf_op jit(solution)/shard_map/ppermute | solution.py:356
  80.0 31.3 %collective-permute-start.3 = (bf16[288,1152]{1,0:T(8,128)(2,1)S(1)}, bf16[288,1152]{1,0:T(8,128)(2,1)S(1)}, u32[]{:S(2)}, u32[]{:S(2)}) collective-permute-start(bf16[288,1152]{1,0:T(8,128)(2,1)S(1)} %get-tuple-element.47), channel_id=1, source_target_pairs={{0,2},{1,3},{2,0},{3,1},{4,6},{5,7},{6,4},{7,5},{8,10},{9,11},{10,... | collective-permute-start | bytes 1990664 | tf_op jit(solution)/shard_map/ppermute | solution.py:356
  82.5 28.9 %collective-permute-start.4 = (bf16[288,1152]{1,0:T(8,128)(2,1)S(1)}, bf16[288,1152]{1,0:T(8,128)(2,1)S(1)}, u32[]{:S(2)}, u32[]{:S(2)}) collective-permute-start(bf16[288,1152]{1,0:T(8,128)(2,1)S(1)} %get-tuple-element.48), channel_id=1, source_target_pairs={{0,3},{1,0},{2,1},{3,2},{4,7},{5,4},{6,5},{7,6},{8,11},{9,8},{10,9... | collective-permute-start | bytes 1990664 | tf_op jit(solution)/shard_map/ppermute | solution.py:356
  83.6 27.7 %collective-permute-start.5 = (bf16[288,1152]{1,0:T(8,128)(2,1)S(1)}, bf16[288,1152]{1,0:T(8,128)(2,1)S(1)}, u32[]{:S(2)}, u32[]{:S(2)}) collective-permute-start(bf16[288,1152]{1,0:T(8,128)(2,1)S(1)} %get-tuple-element.50), channel_id=1, source_target_pairs={{0,32},{16,48},{32,64},{48,80},{64,96},{80,112},{96,0},{112,16},{1... | collective-permute-start | bytes 1990664 | tf_op jit(solution)/shard_map/ppermute | solution.py:352
  83.9 29.9 %collective-permute-start.6 = (bf16[288,1152]{1,0:T(8,128)(2,1)S(1)}, bf16[288,1152]{1,0:T(8,128)(2,1)S(1)}, u32[]{:S(2)}, u32[]{:S(2)}) collective-permute-start(bf16[288,1152]{1,0:T(8,128)(2,1)S(1)} %get-tuple-element.51), channel_id=1, source_target_pairs={{0,64},{16,80},{32,96},{48,112},{64,0},{80,16},{96,32},{112,48},{1... | collective-permute-start | bytes 1990664 | tf_op jit(solution)/shard_map/ppermute | solution.py:352
  96.2 19.3 %collective-permute-start.7 = (bf16[288,1152]{1,0:T(8,128)(2,1)S(1)}, bf16[288,1152]{1,0:T(8,128)(2,1)S(1)}, u32[]{:S(2)}, u32[]{:S(2)}) collective-permute-start(bf16[288,1152]{1,0:T(8,128)(2,1)S(1)} %get-tuple-element.52), channel_id=1, source_target_pairs={{0,96},{16,112},{32,0},{48,16},{64,32},{80,48},{96,64},{112,80},{1... | collective-permute-start | bytes 1990664 | tf_op jit(solution)/shard_map/ppermute | solution.py:352
  116.1 0.7 copy-start.10
  116.8 0.7 copy-start.11
  117.4 6.9 %collective-permute-start.8 = (bf16[72,1152]{1,0:T(8,128)(2,1)S(1)}, bf16[72,1152]{1,0:T(8,128)(2,1)S(1)}, u32[]{:S(2)}, u32[]{:S(2)}) collective-permute-start(bf16[72,1152]{1,0:T(8,128)(2,1)S(1)} %get-tuple-element.54), channel_id=1, source_target_pairs={{0,32},{16,48},{32,64},{48,80},{64,96},{80,112},{96,0},{112,16},{1... | collective-permute-start | bytes 497672 | tf_op jit(solution)/shard_map/ppermute | solution.py:352
  118.8 10.7 %collective-permute-start.9 = (bf16[72,1152]{1,0:T(8,128)(2,1)S(1)}, bf16[72,1152]{1,0:T(8,128)(2,1)S(1)}, u32[]{:S(2)}, u32[]{:S(2)}) collective-permute-start(bf16[72,1152]{1,0:T(8,128)(2,1)S(1)} %get-tuple-element.55), channel_id=1, source_target_pairs={{0,64},{16,80},{32,96},{48,112},{64,0},{80,16},{96,32},{112,48},{1... | collective-permute-start | bytes 497672 | tf_op jit(solution)/shard_map/ppermute | solution.py:352
  122.0 7.4 %collective-permute-start.10 = (bf16[72,1152]{1,0:T(8,128)(2,1)S(1)}, bf16[72,1152]{1,0:T(8,128)(2,1)S(1)}, u32[]{:S(2)}, u32[]{:S(2)}) collective-permute-start(bf16[72,1152]{1,0:T(8,128)(2,1)S(1)} %get-tuple-element.56), channel_id=1, source_target_pairs={{0,96},{16,112},{32,0},{48,16},{64,32},{80,48},{96,64},{112,80},{1... | collective-permute-start | bytes 497672 | tf_op jit(solution)/shard_map/ppermute | solution.py:352
  122.0 10.0 %collective-permute-start.11 = (bf16[72,1152]{1,0:T(8,128)(2,1)S(1)}, bf16[72,1152]{1,0:T(8,128)(2,1)S(1)}, u32[]{:S(2)}, u32[]{:S(2)}) collective-permute-start(bf16[72,1152]{1,0:T(8,128)(2,1)S(1)} %get-tuple-element.58), channel_id=1, source_target_pairs={{0,1},{1,2},{2,3},{3,0},{4,5},{5,6},{6,7},{7,4},{8,9},{9,10},{10,1... | collective-permute-start | bytes 497672 | tf_op jit(solution)/shard_map/ppermute | solution.py:356
  122.2 9.8 %collective-permute-start.12 = (bf16[72,1152]{1,0:T(8,128)(2,1)S(1)}, bf16[72,1152]{1,0:T(8,128)(2,1)S(1)}, u32[]{:S(2)}, u32[]{:S(2)}) collective-permute-start(bf16[72,1152]{1,0:T(8,128)(2,1)S(1)} %get-tuple-element.59), channel_id=1, source_target_pairs={{0,2},{1,3},{2,0},{3,1},{4,6},{5,7},{6,4},{7,5},{8,10},{9,11},{10,... | collective-permute-start | bytes 497672 | tf_op jit(solution)/shard_map/ppermute | solution.py:356
  124.4 7.7 %copy-start.20 = (bf16[72,1152]{1,0:T(8,128)(2,1)}, bf16[72,1152]{1,0:T(8,128)(2,1)S(1)}, u32[]{:S(2)}) copy-start(bf16[72,1152]{1,0:T(8,128)(2,1)S(1)} %collective-permute-done.8.refs_1_) | copy-start | bytes 497668
  124.4 7.7 %collective-permute-start.13 = (bf16[72,1152]{1,0:T(8,128)(2,1)S(1)}, bf16[72,1152]{1,0:T(8,128)(2,1)S(1)}, u32[]{:S(2)}, u32[]{:S(2)}) collective-permute-start(bf16[72,1152]{1,0:T(8,128)(2,1)S(1)} %get-tuple-element.60), channel_id=1, source_target_pairs={{0,3},{1,0},{2,1},{3,2},{4,7},{5,4},{6,5},{7,6},{8,11},{9,8},{10,9... | collective-permute-start | bytes 497672 | tf_op jit(solution)/shard_map/ppermute | solution.py:356
  129.5 2.6 %copy-start.21 = (bf16[72,1152]{1,0:T(8,128)(2,1)}, bf16[72,1152]{1,0:T(8,128)(2,1)S(1)}, u32[]{:S(2)}) copy-start(bf16[72,1152]{1,0:T(8,128)(2,1)S(1)} %collective-permute-done.9.refs_2_) | copy-start | bytes 497668
  129.5 2.6 %copy-start.22 = (bf16[72,1152]{1,0:T(8,128)(2,1)}, bf16[72,1152]{1,0:T(8,128)(2,1)S(1)}, u32[]{:S(2)}) copy-start(bf16[72,1152]{1,0:T(8,128)(2,1)S(1)} %collective-permute-done.10.refs_3_) | copy-start | bytes 497668
  132.1 0.7 copy-start.23
  132.1 0.7 copy-start.24
  132.1 0.8 copy-start.25
  135.1 6.6 %collective-permute-start.14 = (bf16[48,1152]{1,0:T(8,128)(2,1)}, bf16[48,1152]{1,0:T(8,128)(2,1)S(1)}, u32[]{:S(2)}, u32[]{:S(2)}) collective-permute-start(bf16[48,1152]{1,0:T(8,128)(2,1)} %get-tuple-element.62), channel_id=1, source_target_pairs={{0,4},{1,5},{2,6},{3,7},{4,8},{5,9},{6,10},{7,11},{8,12},{9,13},{1... | collective-permute-start | bytes 331784 | tf_op jit(solution)/shard_map/ppermute | solution.py:360
  138.9 8.4 %collective-permute-start.15 = (bf16[48,1152]{1,0:T(8,128)(2,1)}, bf16[48,1152]{1,0:T(8,128)(2,1)S(1)}, u32[]{:S(2)}, u32[]{:S(2)}) collective-permute-start(bf16[48,1152]{1,0:T(8,128)(2,1)} %get-tuple-element.63), channel_id=1, source_target_pairs={{0,8},{1,9},{2,10},{3,11},{4,12},{5,13},{6,14},{7,15},{8,0},{9,1},... | collective-permute-start | bytes 331784 | tf_op jit(solution)/shard_map/ppermute | solution.py:360
  139.4 7.9 %collective-permute-start.16 = (bf16[48,1152]{1,0:T(8,128)(2,1)}, bf16[48,1152]{1,0:T(8,128)(2,1)S(1)}, u32[]{:S(2)}, u32[]{:S(2)}) collective-permute-start(bf16[48,1152]{1,0:T(8,128)(2,1)} %get-tuple-element.64), channel_id=1, source_target_pairs={{0,12},{1,13},{2,14},{3,15},{4,0},{5,1},{6,2},{7,3},{8,4},{9,5},{1... | collective-permute-start | bytes 331784 | tf_op jit(solution)/shard_map/ppermute | solution.py:360
  141.7 5.6 %copy-start.27 = (bf16[48,1152]{1,0:T(8,128)(2,1)}, bf16[48,1152]{1,0:T(8,128)(2,1)S(1)}, u32[]{:S(2)}) copy-start(bf16[48,1152]{1,0:T(8,128)(2,1)S(1)} %collective-permute-done.14.refs_1_) | copy-start | bytes 331780
  147.3 0.6 copy-start.28
  147.3 0.7 copy-start.29
  149.7 8.0 %collective-permute-start.17 = (bf16[48,1152]{1,0:T(8,128)(2,1)}, bf16[48,1152]{1,0:T(8,128)(2,1)S(1)}, u32[]{:S(2)}, u32[]{:S(2)}) collective-permute-start(bf16[48,1152]{1,0:T(8,128)(2,1)} %plain_sum.2.refs_0_), channel_id=1, source_target_pairs={{0,128},{16,144},{32,160},{48,176},{64,192},{80,208},{96,224},{112... | collective-permute-start | bytes 331784 | tf_op jit(solution)/shard_map/ppermute | solution.py:348
  157.7 0.6 copy-start.26
  160.0 3.8 %collective-permute-start.20 = (bf16[48,1152]{1,0:T(8,128)(2,1)}, bf16[48,1152]{1,0:T(8,128)(2,1)S(1)}, u32[]{:S(2)}, u32[]{:S(2)}) collective-permute-start(bf16[48,1152]{1,0:T(8,128)(2,1)} %plain_sum.3), channel_id=1, source_target_pairs={{0,96},{16,112},{32,0},{48,16},{64,32},{80,48},{96,64},{112,80},{1... | collective-permute-start | bytes 331784 | tf_op jit(solution)/shard_map/ppermute | solution.py:352
  160.2 5.4 %collective-permute-start.19 = (bf16[48,1152]{1,0:T(8,128)(2,1)}, bf16[48,1152]{1,0:T(8,128)(2,1)S(1)}, u32[]{:S(2)}, u32[]{:S(2)}) collective-permute-start(bf16[48,1152]{1,0:T(8,128)(2,1)} %plain_sum.3), channel_id=1, source_target_pairs={{0,64},{16,80},{32,96},{48,112},{64,0},{80,16},{96,32},{112,48},{1... | collective-permute-start | bytes 331784 | tf_op jit(solution)/shard_map/ppermute | solution.py:352
  163.2 5.3 %collective-permute-start.18 = (bf16[48,1152]{1,0:T(8,128)(2,1)}, bf16[48,1152]{1,0:T(8,128)(2,1)S(1)}, u32[]{:S(2)}, u32[]{:S(2)}) collective-permute-start(bf16[48,1152]{1,0:T(8,128)(2,1)} %plain_sum.3), channel_id=1, source_target_pairs={{0,32},{16,48},{32,64},{48,80},{64,96},{80,112},{96,0},{112,16},{1... | collective-permute-start | bytes 331784 | tf_op jit(solution)/shard_map/ppermute | solution.py:352
  169.5 6.0 %collective-permute-start.21 = (bf16[4,48,1152]{2,1,0:T(8,128)(2,1)S(1)}, bf16[4,48,1152]{2,1,0:T(8,128)(2,1)S(1)}, u32[]{:S(2)}, u32[]{:S(2)}) collective-permute-start(bf16[4,48,1152]{2,1,0:T(8,128)(2,1)S(1)} %pad_maximum_fusion.mine), channel_id=1, source_target_pairs={{0,16},{16,0},{32,48},{48,32},{64,80},{80,64},{96,112},{112,96},{1... | collective-permute-start | bytes 1327112 | tf_op jit(solution)/shard_map/ppermute | solution.py:344

commit v2 on v1

v2 whole, which is shorter than its diff:
```python
import math

import jax
import jax.numpy as jnp
from jax import lax
from jax.experimental import pallas as pl
from jax.experimental.pallas import tpu as pltpu
from jax.sharding import PartitionSpec as P

HEADS = 16
HEAD_DIM = 72
WINDOW = 8
D = 1152
TOK = 128
CLIPS = 4
REWARDS = 8
ROWS = 16
CHUNK = 384
PIECE = 18
EPS = 1e-06
SCALE = 1.0 / math.sqrt(HEAD_DIM)

f32 = jnp.float32
bf16 = jnp.bfloat16
HI = lax.Precision.HIGHEST
VMEM = pl.BlockSpec(memory_space=pltpu.VMEM)
ANY = pl.BlockSpec(memory_space=pl.ANY)


def dot(a, b, ca, cb, precision=None):
    return lax.dot_general(
        a, b, (((ca,), (cb,)), ((), ())), preferred_element_type=f32, precision=precision
    )


def clip_of(small, frame):
    end, clip = small[10:11, 0:1], jnp.zeros_like(frame)
    for c in range(CLIPS):
        clip += (frame >= end).astype(f32)
        if c + 1 < CLIPS:
            end = end + small[10:11, c + 1 : c + 2]
    return clip


def frames(dims, axis):
    return (lax.broadcasted_iota(jnp.int32, dims, axis) >> 2).astype(f32)


def span(h):
    low = HEAD_DIM * h
    return low // 128 * 128, -(-(low + HEAD_DIM) // 128) * 128


def lane_mask(h):
    start, end = span(h)
    lane = lax.broadcasted_iota(jnp.int32, (1, end - start), 1) + (start - HEAD_DIM * h)
    return ((lane >= 0) & (lane < HEAD_DIM)).astype(f32).astype(bf16)


def standard(values):
    centre = values - jnp.mean(values, axis=-1, keepdims=True)
    inv_std = lax.rsqrt(jnp.mean(centre * centre, axis=-1, keepdims=True) + EPS)
    return centre * inv_std, inv_std


def position():
    tm, dp = lax.axis_index("tm"), lax.axis_index("dp")
    return dp & 3, (tm >> 1) & 3, dp >> 2, tm & 1


def shape(dims, kind):
    return jax.ShapeDtypeStruct(dims, kind)


def call(kernel, out_shape, in_specs, scratch, mib, name, flops=0, moved=0):
    return pl.pallas_call(
        kernel,
        out_shape=out_shape,
        in_specs=in_specs,
        out_specs=jax.tree.map(lambda _: VMEM, out_shape),
        scratch_shapes=scratch,
        compiler_params=pltpu.CompilerParams(vmem_limit_bytes=mib << 20),
        cost_estimate=pl.CostEstimate(flops=flops, bytes_accessed=moved, transcendentals=0),
        name=name,
    )


def regroup_kernel(x_ref, out_ref):
    for q in range(4):
        rows = [x_ref[a, 16 * q : 16 * (q + 1)].astype(f32) for a in range(2)]
        for k in range(4):
            piece = slice(4 * k, 4 * (k + 1))
            out_ref[4 * q + k] = jnp.concatenate([r[piece] for r in rows], axis=0).astype(bf16)


def regroup(tokens):
    return call(
        regroup_kernel, shape((16, 8, D), bf16), [VMEM], [], 4, "regroup", moved=600_000
    )(tokens)


def forward_kernel(
    x_ref, wq_any, wo_any, small,
    normed_ref, attended_ref, proj_ref, p_ref, cen_ref, inv_ref, tot_ref,
    acc, wq_ref, wo_ref, sems,
):
    count = 3 * D // CHUNK
    copies = []
    for j in range(count):
        cols = pl.ds(j * CHUNK, CHUNK)
        copies.append(pltpu.make_async_copy(wq_any.at[:, cols], wq_ref.at[:, cols], sems.at[j]))
    copies.append(pltpu.make_async_copy(wo_any, wo_ref, sems.at[count]))
    for copy in copies:
        copy.start()
    x = x_ref[...].astype(f32)
    norm, _ = standard(x)
    normed = (norm * small[9:10, :]).astype(bf16)
    normed_ref[...] = normed
    for j in range(count):
        copies[j].wait()
        cols = slice(j * CHUNK, (j + 1) * CHUNK)
        proj_ref[:, cols] = dot(normed, wq_ref[:, cols], 1, 0).astype(bf16)
    row = lax.broadcasted_iota(jnp.int32, (TOK, TOK), 0)
    col = lax.broadcasted_iota(jnp.int32, (TOK, TOK), 1)
    lag = (col >> 2) - (row >> 2)
    allowed = (
        ((row & 3) == (col & 3))
        & (lag >= -(WINDOW // 2))
        & (lag < WINDOW - WINDOW // 2)
        & (clip_of(small, frames((TOK, TOK), 0)) == clip_of(small, frames((TOK, TOK), 1)))
    )
    acc[...] = jnp.zeros_like(acc)
    for h in range(HEADS):
        a, b = span(h)
        mask = lane_mask(h)
        logits = dot(proj_ref[:, a:b] * mask, proj_ref[:, D + a : D + b], 1, 1) * SCALE
        masked = jnp.where(allowed, logits, -1e30)
        terms = jnp.exp(masked - jnp.max(masked, axis=1, keepdims=True))
        weights = terms / jnp.sum(terms, axis=1, keepdims=True)
        p_ref[h] = weights
        acc[:, a:b] += dot(
            weights.astype(bf16), proj_ref[:, 2 * D + a : 2 * D + b] * mask, 1, 0
        )
    attended = acc[...].astype(bf16)
    attended_ref[...] = attended
    copies[count].wait()
    mixed = x_ref[...].astype(f32) + dot(attended, wo_ref[...], 1, 0)
    centred, inv_std = standard(mixed)
    cen_ref[...] = centred
    inv_ref[...] = jnp.broadcast_to(inv_std, (TOK, 128))
    final = centred * small[8:9, :]
    clip_row = lax.broadcasted_iota(jnp.int32, (8, TOK), 0).astype(f32)
    onehot = (clip_of(small, frames((8, TOK), 1)) == clip_row).astype(f32)
    tot_ref[...] = dot(dot(onehot, final, 1, 0, HI), small[0:REWARDS, :], 1, 1, HI)


def forward(x, w_qkv, w_out, small):
    return call(
        forward_kernel,
        (
            shape((TOK, D), bf16),
            shape((TOK, D), bf16),
            shape((TOK, 3 * D), bf16),
            shape((HEADS, TOK, TOK), f32),
            shape((TOK, D), f32),
            shape((TOK, 128), f32),
            shape((8, REWARDS), f32),
        ),
        [VMEM, ANY, ANY, VMEM],
        [
            pltpu.VMEM((TOK, D), f32),
            pltpu.VMEM((D, 3 * D), bf16),
            pltpu.VMEM((D, D), bf16),
            pltpu.SemaphoreType.DMA((3 * D // CHUNK + 1,)),
        ],
        48,
        "forward",
        flops=2_000_000_000,
        moved=14_000_000,
    )(x, w_qkv, w_out, small)


def place_rows(src, dst, where, x_first):
    x, y, z, _ = where
    for k in range(64):
        first, second, kz = k // 16, k // 4 % 4, k % 4
        kx, ky = (first, second) if x_first else (second, first)
        dp = ((z + kz) & 3) * 4 + ((x + kx) & 3)
        start = dp * 72 + ((y + ky) & 3) * PIECE
        dst[PIECE * k : PIECE * (k + 1), :] = src[pl.ds(start, PIECE), :]


def turn_kernel(normed_ref, attended_ref, keep_ref, send_ref, turned, placed):
    where = position()
    core = where[3]
    turned[0] = normed_ref[...].astype(f32).T
    turned[1] = attended_ref[...].astype(f32).T
    place_rows(turned.at[0], placed, where, True)
    keep_ref[0] = placed[...].astype(bf16)
    send_ref[0] = keep_ref[0]
    place_rows(turned.at[core], placed, where, False)
    keep_ref[1] = placed[...].astype(bf16)
    place_rows(turned.at[1 - core], placed, where, False)
    send_ref[1] = placed[...].astype(bf16)


def turn(normed, attended):
    return call(
        turn_kernel,
        (shape((2, D, TOK), bf16), shape((2, D, TOK), bf16)),
        [VMEM] * 2,
        [pltpu.VMEM((2, D, TOK), f32), pltpu.VMEM((D, TOK), f32)],
        8,
        "turn",
        moved=4_000_000,
    )(normed, attended)


def backward_kernel(
    t0, t1, t2, t3, small, proj_ref, p_ref, cen_ref, inv_ref, wo_ref,
    scores_ref, keep_ref, send_ref,
    dq, dk, dv, da_ref, res_ref,
):
    clip_row = lax.broadcasted_iota(jnp.int32, (8, REWARDS), 0)
    count = jnp.ones((8, REWARDS), f32)
    for c in range(CLIPS):
        count = jnp.where(clip_row == c, small[10:11, c : c + 1] * 64.0, count)
    scores = ((t0[...] + t2[...]) + (t1[...] + t3[...])) / count
    scores_ref[...] = scores[0:CLIPS]
    res_ref[...] = jnp.zeros_like(res_ref)
    res_ref[0:CLIPS] = (scores[0:CLIPS] - small[12:16, 0:REWARDS]) / ROWS
    clip_grad = dot(res_ref[...], small[0:REWARDS, :], 1, 0, HI) * small[8:9, :]
    clip = lax.broadcasted_iota(jnp.int32, (TOK, 8), 1).astype(f32)
    onehot = (clip_of(small, frames((TOK, 8), 0)) == clip).astype(f32)
    scaled = dot(onehot, clip_grad, 1, 0, HI)
    centred = cen_ref[...]
    mixed_grad = (
        scaled
        - jnp.mean(scaled, axis=-1, keepdims=True)
        - centred * jnp.mean(scaled * centred, axis=-1, keepdims=True)
    ) * inv_ref[:, 0:1]
    mixed_grad = mixed_grad.astype(bf16)
    da_ref[...] = dot(mixed_grad, wo_ref[...], 1, 1).astype(bf16)
    dq[...] = jnp.zeros_like(dq)
    dk[...] = jnp.zeros_like(dk)
    dv[...] = jnp.zeros_like(dv)
    for h in range(HEADS):
        a, b = span(h)
        mask = lane_mask(h)
        out_grad = da_ref[:, a:b] * mask
        weights = p_ref[h]
        weight_grad = dot(out_grad, proj_ref[:, 2 * D + a : 2 * D + b], 1, 1)
        inner = jnp.sum(weights * weight_grad, axis=1, keepdims=True)
        logit_grad = (weights * (weight_grad - inner)).astype(bf16)
        dq[:, a:b] += dot(logit_grad, proj_ref[:, D + a : D + b] * mask, 1, 0)
        dk[:, a:b] += dot(logit_grad, proj_ref[:, a:b] * mask, 0, 0)
        dv[:, a:b] += dot(weights.astype(bf16), out_grad, 0, 0)

    def store(ref_qk, ref_vo):
        ref_qk[0] = (dq[...] * SCALE).astype(bf16)
        ref_qk[1] = (dk[...] * SCALE).astype(bf16)
        ref_vo[0] = dv[...].astype(bf16)
        ref_vo[1] = mixed_grad

    core = position()[3]

    @pl.when(core == 0)
    def _():
        store(keep_ref, send_ref)

    @pl.when(core != 0)
    def _():
        store(send_ref, keep_ref)


def backward(totals, small, proj, p, centred, inv, w_out):
    return call(
        backward_kernel,
        (
            shape((CLIPS, REWARDS), f32),
            shape((2, TOK, D), bf16),
            shape((2, TOK, D), bf16),
        ),
        [VMEM] * 10,
        [pltpu.VMEM((TOK, D), f32)] * 3
        + [
            pltpu.VMEM((TOK, D), bf16),
            pltpu.VMEM((8, REWARDS), f32),
        ],
        16,
        "backward",
        flops=1_500_000_000,
        moved=8_000_000,
    )(*totals, small, proj, p, centred, inv, w_out)


def gradient_kernel(lk, lr, rk, rr, *outs):
    for i in range(2):
        right = jnp.concatenate([rk[i], rr[i]], axis=0)
        for k in range(4):
            rows = slice(288 * k, 288 * (k + 1))
            left = jnp.concatenate([lk[i, rows], lr[i, rows]], axis=1)
            outs[SLOT[i][k]][...] = dot(left, right, 1, 0).astype(bf16)


SLOT = ((0, 3, 6, 5), (1, 2, 7, 4))


def gradient(left_keep, left_recv, right_keep, right_recv):
    return call(
        gradient_kernel,
        (shape((288, D), bf16),) * 8,
        [VMEM] * 4,
        [],
        16,
        "gradient",
        flops=1_400_000_000,
        moved=8_000_000,
    )(left_keep, left_recv, right_keep, right_recv)


def total(refs):
    result = refs[0][...].astype(f32)
    for ref in refs[1:]:
        result += ref[...].astype(f32)
    return result


def first_sum_kernel(*refs):
    for i in range(2):
        result = total([refs[SLOT[i][k]] for k in range(4)])
        for k in range(4):
            refs[8 + SLOT[1 - i][k]][...] = result[72 * k : 72 * (k + 1)].astype(bf16)


def first_sum(parts):
    return call(
        first_sum_kernel,
        (shape((72, D), bf16),) * 8,
        [VMEM] * 8,
        [],
        14,
        "first_sum",
        moved=8_000_000,
    )(*parts)


def second_sum_kernel(*refs):
    sums = [total([refs[SLOT[i][k]] for k in range(4)]) for i in (1, 0)]
    rest = jnp.zeros((4, D), f32)
    for k in range(4):
        rows = slice(PIECE * k, PIECE * (k + 1))
        refs[8 + k][...] = jnp.concatenate([sums[0][rows], sums[1][rows], rest], axis=0).astype(
            bf16
        )


def second_sum(parts):
    return call(
        second_sum_kernel,
        (shape((40, D), bf16),) * 4,
        [VMEM] * 8,
        [],
        6,
        "second_sum",
        moved=1_700_000,
    )(*parts)


def sum_kernel(*refs):
    refs[-1][...] = total(refs[:-1]).astype(bf16)


def plain_sum(parts):
    return call(
        sum_kernel,
        shape(parts[0].shape, bf16),
        [VMEM] * len(parts),
        [],
        3,
        "plain_sum",
        moved=500_000,
    )(*parts)


def last_kernel(*refs):
    qkv_ref, out_ref, held = refs[8:]
    _, y_here, _, core = position()
    for k in range(4):
        y = (y_here - k) & 3
        held[core, y] = refs[k][...].astype(f32)
        held[1 - core, y] = refs[4 + k][...].astype(f32)
    for y in range(4):
        rows = slice(PIECE * y, PIECE * (y + 1))
        qkv_ref[rows, 0:D] = held[0, y, 0:PIECE]
        qkv_ref[rows, D : 2 * D] = held[0, y, PIECE : 2 * PIECE]
        qkv_ref[rows, 2 * D : 3 * D] = held[1, y, 0:PIECE]
        out_ref[rows, :] = held[1, y, PIECE : 2 * PIECE]


def last(parts):
    return call(
        last_kernel,
        (shape((72, 3 * D), f32), shape((72, D), f32)),
        [VMEM] * 8,
        [pltpu.VMEM((2, 4, 40, D), f32)],
        10,
        "last",
        moved=2_000_000,
    )(*parts)


def to_core(block):
    return lax.ppermute(block, "tm", [(i, i ^ 1) for i in range(16)])


def to_far(block, core=0):
    return lax.ppermute(block, "tm", [(i, i ^ 8 ^ core) for i in range(16)])


def along_y(block, k):
    return lax.ppermute(block, "tm", [(i, i & 9 | (i + 2 * k) & 6) for i in range(16)])


def along_x(block, k):
    return lax.ppermute(block, "dp", [(i, i & 12 | (i + k) & 3) for i in range(16)])


def around_z(block, k):
    route = []
    for tm in range(16):
        for dp in range(16):
            step = {1: 1, 3: -1, 2: -2 if tm & 1 else 2}[k]
            z = ((tm >> 3) * 4 + (dp >> 2) + step) & 7
            there = (tm & 7 | (z >> 2) << 3) * 16 + ((z & 3) << 2 | dp & 3)
            route.append((tm * 16 + dp, there))
    return lax.ppermute(block, ("tm", "dp"), route)


def exchange(slots):
    moved = list(slots)
    for k in (1, 3, 2):
        moved[SLOT[1][k]] = along_y(slots[SLOT[1][k]], k)
        moved[SLOT[0][k]] = along_x(slots[SLOT[0][k]], k)
    return moved


def small_arrays(clip_frames, teacher, ln_gain, out_gain, reward_head):
    def wide(block):
        return jnp.pad(block, ((0, 0), (0, D - block.shape[1])))

    return jnp.concatenate(
        [
            reward_head.T,
            out_gain[None],
            ln_gain[None],
            wide(clip_frames.astype(f32)),
            jnp.zeros((1, D), f32),
            wide(teacher),
        ],
        axis=0,
    )


def on_device(tokens, clip_frames, teacher_scores, ln_gain, w_qkv, w_out, out_gain, reward_head):
    x = lax.all_to_all(regroup(tokens[0]), "tm", 0, 0, tiled=True).reshape(TOK, D)
    small = small_arrays(clip_frames, teacher_scores[0], ln_gain, out_gain, reward_head)
    normed, attended, proj, p, centred, inv, partial = forward(x, w_qkv, w_out, small)
    near, far, both = to_core(partial), to_far(partial), to_far(partial, 1)
    partial = (partial + near) + (far + both)
    totals = [partial] + [along_y(partial, k) for k in (1, 2, 3)]
    left_keep, left_send = turn(normed, attended)
    left_recv = to_core(left_send)
    scores, right_keep, right_send = backward(totals, small, proj, p, centred, inv, w_out)
    parts = gradient(left_keep, left_recv, right_keep, to_core(right_send))
    parts = second_sum(exchange(first_sum(exchange(parts))))
    part = plain_sum([parts[0]] + [around_z(parts[k], k) for k in (1, 2, 3)])
    part = plain_sum([part, to_far(part)])
    mine = [part] + [along_y(part, k) for k in (1, 2, 3)]
    qkv_total, out_total = last(mine + [to_core(block) for block in mine])
    return (scores[None], qkv_total, out_total)


def solution(mesh):
    return jax.shard_map(
        on_device,
        mesh=mesh,
        in_specs=(
            P("dp", "tm", None, None),
            P("dp", None),
            P("dp", None, None),
            P(),
            P(),
            P(),
            P(),
            P(),
        ),
        out_specs=(P("dp", None, None), P("dp", None), P("dp", None)),
        check_vma=False,
    )
```

time: 179 us -> 147 us (0.82)
  waiting for transfers between devices: 75.8 us -> 52.4 us
  local copies, waits for them, and re-layouts: 24.5 us -> 5.62 us
  starting transfers between devices: 46.3 us -> 64.4 us
  Pallas kernels: 28.4 us -> 21.6 us
    unnamed x61 -> x4, local copies, waits for them, and re-layouts: 19.1 us -> 2.7 us
    ppermute x4 -> x6, starting transfers between devices: 6.97 us -> 18 us  [the longest x3 9.64 us: to_far(): return lax.ppermute(block, 'tm', [(i, i ^ 8 ^ core) for i in range(16)])]
    ppermute x3 -> x7, starting transfers between devices: 5.21 us -> 15 us  [to_core(): return lax.ppermute(block, 'tm', [(i, i ^ 1) for i in range(16)])]
    all_to_all x2 -> x1, waiting for transfers between devices: 17.3 us -> 7.86 us  [on_device(): lax.all_to_all(regroup(tokens[0]), 'tm', 0, 0, tiled=True).reshape(TOK, D)]
    ppermute x6, waiting for transfers between devices: 27.2 us -> 19.1 us  [along_x(): lax.ppermute(block, 'dp', [(i, i & 12 | i + k & 3) for i in range(16)])]
    pallas_call x8 -> x10, Pallas kernels: 28.4 us -> 21.6 us  [the longest x1 8.69 us: forward(): call(forward_kernel, (shape((TOK, D), bf16), shape((TOK, D), bf16), shape...]
    ppermute x4 -> x6, waiting for transfers between devices: 13.2 us -> 8.32 us  [the longest x3 6 us: to_far(): return lax.ppermute(block, 'tm', [(i, i ^ 8 ^ core) for i in range(16)])]
    all_to_all x2 -> x1, starting transfers between devices: 17.1 us -> 12.6 us  [on_device(): lax.all_to_all(regroup(tokens[0]), 'tm', 0, 0, tiled=True).reshape(TOK, D)]
  transfers between devices with their start and end apart: 24 -> 32, of which waited for: 16 -> 16; matrix products, arithmetic and copies ran while one was open for 2% -> 2% of each run, Pallas kernels for 4% -> 6%
where the time goes in v2:
time: 147 us; the launch traced here: 145 us
  starting transfers between devices  64.4 us (44%)
  waiting for transfers between devices  52.4 us (36%)
  Pallas kernels  21.6 us (15%)
  local copies, waits for them, and re-layouts  5.62 us (4%)
    ppermute x6, waiting for transfers between devices, along_x(): lax.ppermute(block, 'dp', [(i, i & 12 | i + k & 3) for i in range(16)])  19.1 us
    ppermute x7, starting transfers between devices, to_core(): return lax.ppermute(block, 'tm', [(i, i ^ 1) for i in range(16)])  15 us
    ppermute x12, waiting for transfers between devices, along_y(): lax.ppermute(block, 'tm', [(i, i & 9 | i + 2 * k & 6) for i in range(16)])  14.6 us
    all_to_all x1, starting transfers between devices, on_device(): lax.all_to_all(regroup(tokens[0]), 'tm', 0, 0, tiled=True).reshape(TOK, D)  12.6 us
    ppermute x12, starting transfers between devices, along_y(): lax.ppermute(block, 'tm', [(i, i & 9 | i + 2 * k & 6) for i in range(16)])  9.9 us
    ppermute x3, starting transfers between devices, to_far(): return lax.ppermute(block, 'tm', [(i, i ^ 8 ^ core) for i in range(16)])  9.64 us
    ppermute x6, starting transfers between devices, along_x(): lax.ppermute(block, 'dp', [(i, i & 12 | i + k & 3) for i in range(16)])  8.8 us
    pallas_call x1, Pallas kernels, forward(): call(forward_kernel, (shape((TOK, D), bf16), shape((TOK, D), bf16), shape...  8.69 us
  transfers between devices with their start and end apart: 32, of which 16 were waited for; matrix products, arithmetic and copies ran while one was open for 2% of the time, Pallas kernels for 6%

profile of v2, /device:TPU:1, one launch (start us, length us, event | category | flops | bytes accessed | tf_op | source)
XLA Modules:
  0.0 145.4 jit_solution(14675837033718022755)
XLA Ops:
  0.6 1.0 copy-done.1
  1.6 0.8 regroup.1
  2.4 12.6 %all-to-all-start = ((bf16[16,8,1152]{2,1,0:T(8,128)(2,1)}), bf16[16,8,1152]{2,1,0:T(8,128)(2,1)S(1)}, u32[]{:S(2)}, u32[]{:S(2)}) async-start(bf16[16,8,1152]{2,1,0:T(8,128)(2,1)} %regroup.1), calls=%async_computation | async-start | bytes 589824 | tf_op jit(solution)/shard_map/all_to_all | solution.py:466
  15.0 0.7 convert_element_type.7
  15.6 0.7 broadcast_in_dim.13
  16.3 0.7 broadcast_in_dim.12
  17.1 0.7 pad.9
  17.7 0.8 concatenate.3.small
  18.6 7.9 %all-to-all-done = bf16[16,8,1152]{2,1,0:T(8,128)(2,1)S(1)} async-done(((bf16[16,8,1152]{2,1,0:T(8,128)(2,1)}), bf16[16,8,1152]{2,1,0:T(8,128)(2,1)S(1)}, u32[]{:S(2)}, u32[]{:S(2)}) %all-to-all-start) | async-done | bytes 294944 | tf_op jit(solution)/shard_map/all_to_all | solution.py:466
  26.4 1.7 %copy-done = bf16[1152,1152]{1,0:T(8,128)(2,1)S(1)} copy-done((bf16[1152,1152]{1,0:T(8,128)(2,1)S(1)}, bf16[1152,1152]{1,0:T(8,128)(2,1)}, u32[]{:S(2)}) %copy-start) | copy-done | bytes 2654232
  28.2 8.7 %forward.1 = (bf16[128,1152]{1,0:T(8,128)(2,1)S(1)}, bf16[128,1152]{1,0:T(8,128)(2,1)S(1)}, bf16[128,3456]{1,0:T(8,128)(2,1)S(1)}, f32[16,128,128]{2,1,0:T(8,128...) custom-call(bf16[128,1152]{1,0:T(8,128)(2,1)S(1)} %bitcast.5, ...), custom_call_target="tpu_custom_call" | custom-call | flops 2000000000 | bytes 14000000 | tf_op jit(solution)/shard_map/forward/pallas_call | solution.py:158
  36.9 1.3 collective-permute-start.2
  38.2 5.1 %collective-permute-start.1 = (f32[8,8]{1,0:T(8,128)S(1)}, f32[8,8]{1,0:T(8,128)S(1)}, u32[]{:S(2)}, u32[]{:S(2)}) collective-permute-start(f32[8,8]{1,0:T(8,128)S(1)} %get-tuple-element.37), channel_id=1, source_target_pairs={{0,128},{16,144},{32,160},{48,176},{64,192},{80,208},{96,224},{112... | collective-permute-start | bytes 776 | tf_op jit(solution)/shard_map/ppermute | solution.py:418
  43.3 0.6 collective-permute-done.2
  43.9 0.7 collective-permute-done.1
  44.6 0.0 collective-permute-done
  44.6 2.2 %collective-permute-start.5 = (f32[8,8]{1,0:T(8,128)S(1)}, f32[8,8]{1,0:T(8,128)S(1)}, u32[]{:S(2)}, u32[]{:S(2)}) collective-permute-start(f32[8,8]{1,0:T(8,128)S(1)} %add_add_fusion.t0), channel_id=1, source_target_pairs={{0,96},{16,112},{32,0},{48,16},{64,32},{80,48},{96,64},{112,80},{1... | collective-permute-start | bytes 776 | tf_op jit(solution)/shard_map/ppermute | solution.py:422
  46.8 0.0 collective-permute-start.4
  46.8 0.7 collective-permute-start.3
  47.5 0.5 turn.1
  48.0 1.6 %collective-permute-start.6 = (bf16[2,1152,128]{2,1,0:T(8,128)(2,1)S(1)}, bf16[2,1152,128]{2,1,0:T(8,128)(2,1)S(1)}, u32[]{:S(2)}, u32[]{:S(2)}) collective-permute-start(bf16[2,1152,128]{2,1,0:T(8,128)(2,1)S(1)} %get-tuple-element.46), channel_id=1, source_target_pairs={{0,16},{16,0},{32,48},{48,32},{64,80},{80,64},{96,112},{112,96},{1... | collective-permute-start | bytes 1769480 | tf_op jit(solution)/shard_map/ppermute | solution.py:414
  49.5 1.2 collective-permute-done.4.t2
  50.7 7.6 %backward.1 = (f32[4,8]{1,0:T(4,128)}, bf16[2,128,1152]{2,1,0:T(8,128)(2,1)S(1)}, bf16[2,128,1152]{2,1,0:T(8,128)(2,1)S(1)}) custom-call(f32[8,8]{1,0:T(8,128)S(1)} %add_add_fusion.t0, f32[8,8]{1,0:T(8,128)S(1)} %collective-permute-done.3.t1, f32[8,8]{1,0:T(8,128)S(1)} %collective-permute-done.4.t2, f32[8,8]{1,0:T(8,128)S(1)} %collective-permute-done.5.t3, ...), custom_call_target="tpu_custom_call" | custom-call | flops 1500000000 | bytes 8000000 | tf_op jit(solution)/shard_map/backward/pallas_call | solution.py:277
  58.4 2.3 %collective-permute-start.7 = (bf16[2,128,1152]{2,1,0:T(8,128)(2,1)S(1)}, bf16[2,128,1152]{2,1,0:T(8,128)(2,1)S(1)}, u32[]{:S(2)}, u32[]{:S(2)}) collective-permute-start(bf16[2,128,1152]{2,1,0:T(8,128)(2,1)S(1)} %get-tuple-element.48), channel_id=1, source_target_pairs={{0,16},{16,0},{32,48},{48,32},{64,80},{80,64},{96,112},{112,96},{1... | collective-permute-start | bytes 1769480 | tf_op jit(solution)/shard_map/ppermute | solution.py:414
  60.7 0.0 collective-permute-done.6.lr
  60.7 1.6 %collective-permute-done.7.rr = bf16[2,128,1152]{2,1,0:T(8,128)(2,1)S(1)} collective-permute-done((bf16[2,128,1152]{2,1,0:T(8,128)(2,1)S(1)}, bf16[2,128,1152]{2,1,0:T(8,128)(2,1)S(1)}, u32[]{:S(2)}, u32[]{:S(2)}) %collective-permute-start.7) | collective-permute-done | bytes 589856 | tf_op jit(solution)/shard_map/ppermute | solution.py:414
  62.3 1.7 %gradient.1 = (bf16[288,1152]{1,0:T(8,128)(2,1)S(1)}, bf16[288,1152]{1,0:T(8,128)(2,1)S(1)}, bf16[288,1152]{1,0:T(8,128)(2,1)S(1)}, bf16[288,1152]{1,0:T(8,128)(...) custom-call(bf16[2,1152,128]{2,1,0:T(8,128)(2,1)S(1)} %get-tuple-ele, ...), custom_call_target="tpu_custom_call" | custom-call | flops 1400000000 | bytes 8000000 | tf_op jit(solution)/shard_map/gradient/pallas_call | solution.py:310
  64.0 0.1 collective-permute-start.8
  64.1 1.3 collective-permute-start.9
  65.4 2.6 %collective-permute-start.10 = (bf16[288,1152]{1,0:T(8,128)(2,1)S(1)}, bf16[288,1152]{1,0:T(8,128)(2,1)S(1)}, u32[]{:S(2)}, u32[]{:S(2)}) collective-permute-start(bf16[288,1152]{1,0:T(8,128)(2,1)S(1)} %get-tuple-element.53), channel_id=1, source_target_pairs={{0,96},{16,112},{32,0},{48,16},{64,32},{80,48},{96,64},{112,80},{1... | collective-permute-start | bytes 1990664 | tf_op jit(solution)/shard_map/ppermute | solution.py:422
  68.0 1.5 %collective-permute-start.11 = (bf16[288,1152]{1,0:T(8,128)(2,1)S(1)}, bf16[288,1152]{1,0:T(8,128)(2,1)S(1)}, u32[]{:S(2)}, u32[]{:S(2)}) collective-permute-start(bf16[288,1152]{1,0:T(8,128)(2,1)S(1)} %get-tuple-element.54), channel_id=1, source_target_pairs={{0,3},{1,0},{2,1},{3,2},{4,7},{5,4},{6,5},{7,6},{8,11},{9,8},{10,9... | collective-permute-start | bytes 1990664 | tf_op jit(solution)/shard_map/ppermute | solution.py:426
  69.5 1.5 %collective-permute-start.12 = (bf16[288,1152]{1,0:T(8,128)(2,1)S(1)}, bf16[288,1152]{1,0:T(8,128)(2,1)S(1)}, u32[]{:S(2)}, u32[]{:S(2)}) collective-permute-start(bf16[288,1152]{1,0:T(8,128)(2,1)S(1)} %get-tuple-element.55), channel_id=1, source_target_pairs={{0,2},{1,3},{2,0},{3,1},{4,6},{5,7},{6,4},{7,5},{8,10},{9,11},{10,... | collective-permute-start | bytes 1990664 | tf_op jit(solution)/shard_map/ppermute | solution.py:426
  71.0 10.4 %collective-permute-done.8.refs_2_ = bf16[288,1152]{1,0:T(8,128)(2,1)S(1)} collective-permute-done((bf16[288,1152]{1,0:T(8,128)(2,1)S(1)}, bf16[288,1152]{1,0:T(8,128)(2,1)S(1)}, u32[]{:S(2)}, u32[]{:S(2)}) %collective-permute-start.8) | collective-permute-done | bytes 663584 | tf_op jit(solution)/shard_map/ppermute | solution.py:422
  81.5 0.4 collective-permute-start.13
  81.8 1.4 collective-permute-done.11.refs_5_
  83.2 13.6 %collective-permute-done.12.refs_6_ = bf16[288,1152]{1,0:T(8,128)(2,1)S(1)} collective-permute-done((bf16[288,1152]{1,0:T(8,128)(2,1)S(1)}, bf16[288,1152]{1,0:T(8,128)(2,1)S(1)}, u32[]{:S(2)}, u32[]{:S(2)}) %collective-permute-start.12) | collective-permute-done | bytes 663584 | tf_op jit(solution)/shard_map/ppermute | solution.py:426
  96.8 1.4 collective-permute-done.13.refs_7_
  98.2 0.7 first_sum.1
  98.8 0.1 collective-permute-start.14
  98.9 1.5 %collective-permute-start.15 = (bf16[72,1152]{1,0:T(8,128)(2,1)S(1)}, bf16[72,1152]{1,0:T(8,128)(2,1)S(1)}, u32[]{:S(2)}, u32[]{:S(2)}) collective-permute-start(bf16[72,1152]{1,0:T(8,128)(2,1)S(1)} %get-tuple-element.60), channel_id=1, source_target_pairs={{0,1},{1,2},{2,3},{3,0},{4,5},{5,6},{6,7},{7,4},{8,9},{9,10},{10,1... | collective-permute-start | bytes 497672 | tf_op jit(solution)/shard_map/ppermute | solution.py:426
  100.4 2.4 %collective-permute-start.16 = (bf16[72,1152]{1,0:T(8,128)(2,1)S(1)}, bf16[72,1152]{1,0:T(8,128)(2,1)S(1)}, u32[]{:S(2)}, u32[]{:S(2)}) collective-permute-start(bf16[72,1152]{1,0:T(8,128)(2,1)S(1)} %get-tuple-element.61), channel_id=1, source_target_pairs={{0,96},{16,112},{32,0},{48,16},{64,32},{80,48},{96,64},{112,80},{1... | collective-permute-start | bytes 497672 | tf_op jit(solution)/shard_map/ppermute | solution.py:422
  102.8 1.5 %collective-permute-start.17 = (bf16[72,1152]{1,0:T(8,128)(2,1)S(1)}, bf16[72,1152]{1,0:T(8,128)(2,1)S(1)}, u32[]{:S(2)}, u32[]{:S(2)}) collective-permute-start(bf16[72,1152]{1,0:T(8,128)(2,1)S(1)} %get-tuple-element.62), channel_id=1, source_target_pairs={{0,3},{1,0},{2,1},{3,2},{4,7},{5,4},{6,5},{7,6},{8,11},{9,8},{10,9... | collective-permute-start | bytes 497672 | tf_op jit(solution)/shard_map/ppermute | solution.py:426
  104.3 1.5 %collective-permute-start.18 = (bf16[72,1152]{1,0:T(8,128)(2,1)S(1)}, bf16[72,1152]{1,0:T(8,128)(2,1)S(1)}, u32[]{:S(2)}, u32[]{:S(2)}) collective-permute-start(bf16[72,1152]{1,0:T(8,128)(2,1)S(1)} %get-tuple-element.63), channel_id=1, source_target_pairs={{0,2},{1,3},{2,0},{3,1},{4,6},{5,7},{6,4},{7,5},{8,10},{9,11},{10,... | collective-permute-start | bytes 497672 | tf_op jit(solution)/shard_map/ppermute | solution.py:426
  105.8 1.5 %collective-permute-done.17.refs_5_ = bf16[72,1152]{1,0:T(8,128)(2,1)S(1)} collective-permute-done((bf16[72,1152]{1,0:T(8,128)(2,1)S(1)}, bf16[72,1152]{1,0:T(8,128)(2,1)S(1)}, u32[]{:S(2)}, u32[]{:S(2)}) %collective-permute-start.17) | collective-permute-done | bytes 165920 | tf_op jit(solution)/shard_map/ppermute | solution.py:426
  107.3 2.7 %collective-permute-done.18.refs_6_ = bf16[72,1152]{1,0:T(8,128)(2,1)S(1)} collective-permute-done((bf16[72,1152]{1,0:T(8,128)(2,1)S(1)}, bf16[72,1152]{1,0:T(8,128)(2,1)S(1)}, u32[]{:S(2)}, u32[]{:S(2)}) %collective-permute-start.18) | collective-permute-done | bytes 165920 | tf_op jit(solution)/shard_map/ppermute | solution.py:426
  110.0 1.5 %collective-permute-done.19.refs_7_ = bf16[72,1152]{1,0:T(8,128)(2,1)S(1)} collective-permute-done((bf16[72,1152]{1,0:T(8,128)(2,1)S(1)}, bf16[72,1152]{1,0:T(8,128)(2,1)S(1)}, u32[]{:S(2)}, u32[]{:S(2)}) %collective-permute-start.19) | collective-permute-done | bytes 165920 | tf_op jit(solution)/shard_map/ppermute | solution.py:422
  111.5 0.2 second_sum.1
  111.7 3.5 %collective-permute-start.20 = (bf16[40,1152]{1,0:T(8,128)(2,1)S(1)}, bf16[40,1152]{1,0:T(8,128)(2,1)S(1)}, u32[]{:S(2)}, u32[]{:S(2)}) collective-permute-start(bf16[40,1152]{1,0:T(8,128)(2,1)S(1)} %get-tuple-element.66), channel_id=1, source_target_pairs={{0,4},{1,5},{2,6},{3,7},{4,8},{5,9},{6,10},{7,11},{8,12},{9,13},{1... | collective-permute-start | bytes 276488 | tf_op jit(solution)/shard_map/ppermute | solution.py:437
  115.2 3.6 %collective-permute-start.21 = (bf16[40,1152]{1,0:T(8,128)(2,1)S(1)}, bf16[40,1152]{1,0:T(8,128)(2,1)S(1)}, u32[]{:S(2)}, u32[]{:S(2)}) collective-permute-start(bf16[40,1152]{1,0:T(8,128)(2,1)S(1)} %get-tuple-element.67), channel_id=1, source_target_pairs={{0,8},{1,9},{2,10},{3,11},{4,12},{5,13},{6,14},{7,15},{8,128},{9,1... | collective-permute-start | bytes 276488 | tf_op jit(solution)/shard_map/ppermute | solution.py:437
  118.7 1.4 collective-permute-start.22
  120.1 0.4 collective-permute-done.21.refs_2_
  120.5 2.0 %collective-permute-done.22.refs_3_ = bf16[40,1152]{1,0:T(8,128)(2,1)S(1)} collective-permute-done((bf16[40,1152]{1,0:T(8,128)(2,1)S(1)}, bf16[40,1152]{1,0:T(8,128)(2,1)S(1)}, u32[]{:S(2)}, u32[]{:S(2)}) %collective-permute-start.22) | collective-permute-done | bytes 92192 | tf_op jit(solution)/shard_map/ppermute | solution.py:437
  122.4 0.1 plain_sum.2.refs_0_
  122.5 3.2 %collective-permute-start.23 = (bf16[40,1152]{1,0:T(8,128)(2,1)S(1)}, bf16[40,1152]{1,0:T(8,128)(2,1)S(1)}, u32[]{:S(2)}, u32[]{:S(2)}) collective-permute-start(bf16[40,1152]{1,0:T(8,128)(2,1)S(1)} %plain_sum.2.refs_0_), channel_id=1, source_target_pairs={{0,128},{16,144},{32,160},{48,176},{64,192},{80,208},{96,224},{112... | collective-permute-start | bytes 276488 | tf_op jit(solution)/shard_map/ppermute | solution.py:418
  125.7 4.7 %collective-permute-done.23.refs_1_ = bf16[40,1152]{1,0:T(8,128)(2,1)S(1)} collective-permute-done((bf16[40,1152]{1,0:T(8,128)(2,1)S(1)}, bf16[40,1152]{1,0:T(8,128)(2,1)S(1)}, u32[]{:S(2)}, u32[]{:S(2)}) %collective-permute-start.23) | collective-permute-done | bytes 92192 | tf_op jit(solution)/shard_map/ppermute | solution.py:418
  130.5 0.3 collective-permute-start.26
  130.8 0.9 collective-permute-start.25
  131.7 0.3 collective-permute-start.24
  132.0 6.0 %collective-permute-start.27 = (bf16[40,1152]{1,0:T(8,128)(2,1)S(1)}, bf16[40,1152]{1,0:T(8,128)(2,1)S(1)}, u32[]{:S(2)}, u32[]{:S(2)}) collective-permute-start(bf16[40,1152]{1,0:T(8,128)(2,1)S(1)} %plain_sum.3.refs_0_), channel_id=1, source_target_pairs={{0,16},{16,0},{32,48},{48,32},{64,80},{80,64},{96,112},{112,96},{1... | collective-permute-start | bytes 276488 | tf_op jit(solution)/shard_map/ppermute | solution.py:414
  138.0 2.5 %collective-permute-start.30 = (bf16[40,1152]{1,0:T(8,128)(2,1)S(1)}, bf16[40,1152]{1,0:T(8,128)(2,1)S(1)}, u32[]{:S(2)}, u32[]{:S(2)}) collective-permute-start(bf16[40,1152]{1,0:T(8,128)(2,1)S(1)} %collective-permute-done.26.refs_3_), channel_id=1, source_target_pairs={{0,16},{16,0},{32,48},{48,32},{64,80},{80,64},{96,112},{112,96},{1... | collective-permute-start | bytes 276488 | tf_op jit(solution)/shard_map/ppermute | solution.py:414
  140.5 1.6 %collective-permute-start.29 = (bf16[40,1152]{1,0:T(8,128)(2,1)S(1)}, bf16[40,1152]{1,0:T(8,128)(2,1)S(1)}, u32[]{:S(2)}, u32[]{:S(2)}) collective-permute-start(bf16[40,1152]{1,0:T(8,128)(2,1)S(1)} %collective-permute-done.25.refs_2_), channel_id=1, source_target_pairs={{0,16},{16,0},{32,48},{48,32},{64,80},{80,64},{96,112},{112,96},{1... | collective-permute-start | bytes 276488 | tf_op jit(solution)/shard_map/ppermute | solution.py:414
  142.1 1.1 collective-permute-start.28
  143.2 0.9 collective-permute-done.28.refs_5_
  144.1 1.3 last.1
  (22 shorter events, 0.1 us)
Async XLA Ops:
  0.6 1.0 copy-start.1
  2.4 24.1 %all-to-all-start = ((bf16[16,8,1152]{2,1,0:T(8,128)(2,1)}), bf16[16,8,1152]{2,1,0:T(8,128)(2,1)S(1)}, u32[]{:S(2)}, u32[]{:S(2)}) async-start(bf16[16,8,1152]{2,1,0:T(8,128)(2,1)} %regroup.1), calls=%async_computation | async-start | bytes 589824 | tf_op jit(solution)/shard_map/all_to_all | solution.py:466
  26.4 1.8 %copy-start = (bf16[1152,1152]{1,0:T(8,128)(2,1)S(1)}, bf16[1152,1152]{1,0:T(8,128)(2,1)}, u32[]{:S(2)}) copy-start(bf16[1152,1152]{1,0:T(8,128)(2,1)} %wo_ref.1) | copy-start | bytes 7962628
  36.9 7.0 %collective-permute-start.2 = (f32[8,8]{1,0:T(8,128)S(1)}, f32[8,8]{1,0:T(8,128)S(1)}, u32[]{:S(2)}, u32[]{:S(2)}) collective-permute-start(f32[8,8]{1,0:T(8,128)S(1)} %get-tuple-element.37), channel_id=1, source_target_pairs={{0,144},{16,128},{32,176},{48,160},{64,208},{80,192},{96,240},{112... | collective-permute-start | bytes 776 | tf_op jit(solution)/shard_map/ppermute | solution.py:418
  38.2 6.4 %collective-permute-start.1 = (f32[8,8]{1,0:T(8,128)S(1)}, f32[8,8]{1,0:T(8,128)S(1)}, u32[]{:S(2)}, u32[]{:S(2)}) collective-permute-start(f32[8,8]{1,0:T(8,128)S(1)} %get-tuple-element.37), channel_id=1, source_target_pairs={{0,128},{16,144},{32,160},{48,176},{64,192},{80,208},{96,224},{112... | collective-permute-start | bytes 776 | tf_op jit(solution)/shard_map/ppermute | solution.py:418
  43.3 1.3 collective-permute-start
  44.6 4.9 %collective-permute-start.5 = (f32[8,8]{1,0:T(8,128)S(1)}, f32[8,8]{1,0:T(8,128)S(1)}, u32[]{:S(2)}, u32[]{:S(2)}) collective-permute-start(f32[8,8]{1,0:T(8,128)S(1)} %add_add_fusion.t0), channel_id=1, source_target_pairs={{0,96},{16,112},{32,0},{48,16},{64,32},{80,48},{96,64},{112,80},{1... | collective-permute-start | bytes 776 | tf_op jit(solution)/shard_map/ppermute | solution.py:422
  46.8 4.0 %collective-permute-start.4 = (f32[8,8]{1,0:T(8,128)S(1)}, f32[8,8]{1,0:T(8,128)S(1)}, u32[]{:S(2)}, u32[]{:S(2)}) collective-permute-start(f32[8,8]{1,0:T(8,128)S(1)} %add_add_fusion.t0), channel_id=1, source_target_pairs={{0,64},{16,80},{32,96},{48,112},{64,0},{80,16},{96,32},{112,48},{1... | collective-permute-start | bytes 776 | tf_op jit(solution)/shard_map/ppermute | solution.py:422
  46.8 4.0 %collective-permute-start.3 = (f32[8,8]{1,0:T(8,128)S(1)}, f32[8,8]{1,0:T(8,128)S(1)}, u32[]{:S(2)}, u32[]{:S(2)}) collective-permute-start(f32[8,8]{1,0:T(8,128)S(1)} %add_add_fusion.t0), channel_id=1, source_target_pairs={{0,32},{16,48},{32,64},{48,80},{64,96},{80,112},{96,0},{112,16},{1... | collective-permute-start | bytes 776 | tf_op jit(solution)/shard_map/ppermute | solution.py:422
  48.0 12.8 %collective-permute-start.6 = (bf16[2,1152,128]{2,1,0:T(8,128)(2,1)S(1)}, bf16[2,1152,128]{2,1,0:T(8,128)(2,1)S(1)}, u32[]{:S(2)}, u32[]{:S(2)}) collective-permute-start(bf16[2,1152,128]{2,1,0:T(8,128)(2,1)S(1)} %get-tuple-element.46), channel_id=1, source_target_pairs={{0,16},{16,0},{32,48},{48,32},{64,80},{80,64},{96,112},{112,96},{1... | collective-permute-start | bytes 1769480 | tf_op jit(solution)/shard_map/ppermute | solution.py:414
  58.4 4.0 %collective-permute-start.7 = (bf16[2,128,1152]{2,1,0:T(8,128)(2,1)S(1)}, bf16[2,128,1152]{2,1,0:T(8,128)(2,1)S(1)}, u32[]{:S(2)}, u32[]{:S(2)}) collective-permute-start(bf16[2,128,1152]{2,1,0:T(8,128)(2,1)S(1)} %get-tuple-element.48), channel_id=1, source_target_pairs={{0,16},{16,0},{32,48},{48,32},{64,80},{80,64},{96,112},{112,96},{1... | collective-permute-start | bytes 1769480 | tf_op jit(solution)/shard_map/ppermute | solution.py:414
  64.0 17.4 %collective-permute-start.8 = (bf16[288,1152]{1,0:T(8,128)(2,1)S(1)}, bf16[288,1152]{1,0:T(8,128)(2,1)S(1)}, u32[]{:S(2)}, u32[]{:S(2)}) collective-permute-start(bf16[288,1152]{1,0:T(8,128)(2,1)S(1)} %get-tuple-element.51), channel_id=1, source_target_pairs={{0,32},{16,48},{32,64},{48,80},{64,96},{80,112},{96,0},{112,16},{1... | collective-permute-start | bytes 1990664 | tf_op jit(solution)/shard_map/ppermute | solution.py:422
  64.1 17.7 %collective-permute-start.9 = (bf16[288,1152]{1,0:T(8,128)(2,1)S(1)}, bf16[288,1152]{1,0:T(8,128)(2,1)S(1)}, u32[]{:S(2)}, u32[]{:S(2)}) collective-permute-start(bf16[288,1152]{1,0:T(8,128)(2,1)S(1)} %get-tuple-element.52), channel_id=1, source_target_pairs={{0,1},{1,2},{2,3},{3,0},{4,5},{5,6},{6,7},{7,4},{8,9},{9,10},{10,1... | collective-permute-start | bytes 1990664 | tf_op jit(solution)/shard_map/ppermute | solution.py:426
  65.4 16.4 %collective-permute-start.10 = (bf16[288,1152]{1,0:T(8,128)(2,1)S(1)}, bf16[288,1152]{1,0:T(8,128)(2,1)S(1)}, u32[]{:S(2)}, u32[]{:S(2)}) collective-permute-start(bf16[288,1152]{1,0:T(8,128)(2,1)S(1)} %get-tuple-element.53), channel_id=1, source_target_pairs={{0,96},{16,112},{32,0},{48,16},{64,32},{80,48},{96,64},{112,80},{1... | collective-permute-start | bytes 1990664 | tf_op jit(solution)/shard_map/ppermute | solution.py:422
  68.0 15.2 %collective-permute-start.11 = (bf16[288,1152]{1,0:T(8,128)(2,1)S(1)}, bf16[288,1152]{1,0:T(8,128)(2,1)S(1)}, u32[]{:S(2)}, u32[]{:S(2)}) collective-permute-start(bf16[288,1152]{1,0:T(8,128)(2,1)S(1)} %get-tuple-element.54), channel_id=1, source_target_pairs={{0,3},{1,0},{2,1},{3,2},{4,7},{5,4},{6,5},{7,6},{8,11},{9,8},{10,9... | collective-permute-start | bytes 1990664 | tf_op jit(solution)/shard_map/ppermute | solution.py:426
  69.5 27.3 %collective-permute-start.12 = (bf16[288,1152]{1,0:T(8,128)(2,1)S(1)}, bf16[288,1152]{1,0:T(8,128)(2,1)S(1)}, u32[]{:S(2)}, u32[]{:S(2)}) collective-permute-start(bf16[288,1152]{1,0:T(8,128)(2,1)S(1)} %get-tuple-element.55), channel_id=1, source_target_pairs={{0,2},{1,3},{2,0},{3,1},{4,6},{5,7},{6,4},{7,5},{8,10},{9,11},{10,... | collective-permute-start | bytes 1990664 | tf_op jit(solution)/shard_map/ppermute | solution.py:426
  81.5 16.7 %collective-permute-start.13 = (bf16[288,1152]{1,0:T(8,128)(2,1)S(1)}, bf16[288,1152]{1,0:T(8,128)(2,1)S(1)}, u32[]{:S(2)}, u32[]{:S(2)}) collective-permute-start(bf16[288,1152]{1,0:T(8,128)(2,1)S(1)} %get-tuple-element.56), channel_id=1, source_target_pairs={{0,64},{16,80},{32,96},{48,112},{64,0},{80,16},{96,32},{112,48},{1... | collective-permute-start | bytes 1990664 | tf_op jit(solution)/shard_map/ppermute | solution.py:422
  98.8 7.0 %collective-permute-start.14 = (bf16[72,1152]{1,0:T(8,128)(2,1)S(1)}, bf16[72,1152]{1,0:T(8,128)(2,1)S(1)}, u32[]{:S(2)}, u32[]{:S(2)}) collective-permute-start(bf16[72,1152]{1,0:T(8,128)(2,1)S(1)} %get-tuple-element.59), channel_id=1, source_target_pairs={{0,32},{16,48},{32,64},{48,80},{64,96},{80,112},{96,0},{112,16},{1... | collective-permute-start | bytes 497672 | tf_op jit(solution)/shard_map/ppermute | solution.py:422
  98.9 6.9 %collective-permute-start.15 = (bf16[72,1152]{1,0:T(8,128)(2,1)S(1)}, bf16[72,1152]{1,0:T(8,128)(2,1)S(1)}, u32[]{:S(2)}, u32[]{:S(2)}) collective-permute-start(bf16[72,1152]{1,0:T(8,128)(2,1)S(1)} %get-tuple-element.60), channel_id=1, source_target_pairs={{0,1},{1,2},{2,3},{3,0},{4,5},{5,6},{6,7},{7,4},{8,9},{9,10},{10,1... | collective-permute-start | bytes 497672 | tf_op jit(solution)/shard_map/ppermute | solution.py:426
  100.4 5.4 %collective-permute-start.16 = (bf16[72,1152]{1,0:T(8,128)(2,1)S(1)}, bf16[72,1152]{1,0:T(8,128)(2,1)S(1)}, u32[]{:S(2)}, u32[]{:S(2)}) collective-permute-start(bf16[72,1152]{1,0:T(8,128)(2,1)S(1)} %get-tuple-element.61), channel_id=1, source_target_pairs={{0,96},{16,112},{32,0},{48,16},{64,32},{80,48},{96,64},{112,80},{1... | collective-permute-start | bytes 497672 | tf_op jit(solution)/shard_map/ppermute | solution.py:422
  102.8 4.5 %collective-permute-start.17 = (bf16[72,1152]{1,0:T(8,128)(2,1)S(1)}, bf16[72,1152]{1,0:T(8,128)(2,1)S(1)}, u32[]{:S(2)}, u32[]{:S(2)}) collective-permute-start(bf16[72,1152]{1,0:T(8,128)(2,1)S(1)} %get-tuple-element.62), channel_id=1, source_target_pairs={{0,3},{1,0},{2,1},{3,2},{4,7},{5,4},{6,5},{7,6},{8,11},{9,8},{10,9... | collective-permute-start | bytes 497672 | tf_op jit(solution)/shard_map/ppermute | solution.py:426
  104.3 5.7 %collective-permute-start.18 = (bf16[72,1152]{1,0:T(8,128)(2,1)S(1)}, bf16[72,1152]{1,0:T(8,128)(2,1)S(1)}, u32[]{:S(2)}, u32[]{:S(2)}) collective-permute-start(bf16[72,1152]{1,0:T(8,128)(2,1)S(1)} %get-tuple-element.63), channel_id=1, source_target_pairs={{0,2},{1,3},{2,0},{3,1},{4,6},{5,7},{6,4},{7,5},{8,10},{9,11},{10,... | collective-permute-start | bytes 497672 | tf_op jit(solution)/shard_map/ppermute | solution.py:426
  105.8 5.7 %collective-permute-start.19 = (bf16[72,1152]{1,0:T(8,128)(2,1)S(1)}, bf16[72,1152]{1,0:T(8,128)(2,1)S(1)}, u32[]{:S(2)}, u32[]{:S(2)}) collective-permute-start(bf16[72,1152]{1,0:T(8,128)(2,1)S(1)} %get-tuple-element.64), channel_id=1, source_target_pairs={{0,64},{16,80},{32,96},{48,112},{64,0},{80,16},{96,32},{112,48},{1... | collective-permute-start | bytes 497672 | tf_op jit(solution)/shard_map/ppermute | solution.py:422
  111.7 8.4 %collective-permute-start.20 = (bf16[40,1152]{1,0:T(8,128)(2,1)S(1)}, bf16[40,1152]{1,0:T(8,128)(2,1)S(1)}, u32[]{:S(2)}, u32[]{:S(2)}) collective-permute-start(bf16[40,1152]{1,0:T(8,128)(2,1)S(1)} %get-tuple-element.66), channel_id=1, source_target_pairs={{0,4},{1,5},{2,6},{3,7},{4,8},{5,9},{6,10},{7,11},{8,12},{9,13},{1... | collective-permute-start | bytes 276488 | tf_op jit(solution)/shard_map/ppermute | solution.py:437
  115.2 5.3 %collective-permute-start.21 = (bf16[40,1152]{1,0:T(8,128)(2,1)S(1)}, bf16[40,1152]{1,0:T(8,128)(2,1)S(1)}, u32[]{:S(2)}, u32[]{:S(2)}) collective-permute-start(bf16[40,1152]{1,0:T(8,128)(2,1)S(1)} %get-tuple-element.67), channel_id=1, source_target_pairs={{0,8},{1,9},{2,10},{3,11},{4,12},{5,13},{6,14},{7,15},{8,128},{9,1... | collective-permute-start | bytes 276488 | tf_op jit(solution)/shard_map/ppermute | solution.py:437
  118.7 3.7 %collective-permute-start.22 = (bf16[40,1152]{1,0:T(8,128)(2,1)S(1)}, bf16[40,1152]{1,0:T(8,128)(2,1)S(1)}, u32[]{:S(2)}, u32[]{:S(2)}) collective-permute-start(bf16[40,1152]{1,0:T(8,128)(2,1)S(1)} %get-tuple-element.68), channel_id=1, source_target_pairs={{0,140},{1,141},{2,142},{3,143},{4,0},{5,1},{6,2},{7,3},{8,4},{9,5... | collective-permute-start | bytes 276488 | tf_op jit(solution)/shard_map/ppermute | solution.py:437
  122.5 7.9 %collective-permute-start.23 = (bf16[40,1152]{1,0:T(8,128)(2,1)S(1)}, bf16[40,1152]{1,0:T(8,128)(2,1)S(1)}, u32[]{:S(2)}, u32[]{:S(2)}) collective-permute-start(bf16[40,1152]{1,0:T(8,128)(2,1)S(1)} %plain_sum.2.refs_0_), channel_id=1, source_target_pairs={{0,128},{16,144},{32,160},{48,176},{64,192},{80,208},{96,224},{112... | collective-permute-start | bytes 276488 | tf_op jit(solution)/shard_map/ppermute | solution.py:418
  130.5 7.5 %collective-permute-start.26 = (bf16[40,1152]{1,0:T(8,128)(2,1)S(1)}, bf16[40,1152]{1,0:T(8,128)(2,1)S(1)}, u32[]{:S(2)}, u32[]{:S(2)}) collective-permute-start(bf16[40,1152]{1,0:T(8,128)(2,1)S(1)} %plain_sum.3.refs_0_), channel_id=1, source_target_pairs={{0,96},{16,112},{32,0},{48,16},{64,32},{80,48},{96,64},{112,80},{1... | collective-permute-start | bytes 276488 | tf_op jit(solution)/shard_map/ppermute | solution.py:422
  130.8 9.7 %collective-permute-start.25 = (bf16[40,1152]{1,0:T(8,128)(2,1)S(1)}, bf16[40,1152]{1,0:T(8,128)(2,1)S(1)}, u32[]{:S(2)}, u32[]{:S(2)}) collective-permute-start(bf16[40,1152]{1,0:T(8,128)(2,1)S(1)} %plain_sum.3.refs_0_), channel_id=1, source_target_pairs={{0,64},{16,80},{32,96},{48,112},{64,0},{80,16},{96,32},{112,48},{1... | collective-permute-start | bytes 276488 | tf_op jit(solution)/shard_map/ppermute | solution.py:422
  131.7 10.4 %collective-permute-start.24 = (bf16[40,1152]{1,0:T(8,128)(2,1)S(1)}, bf16[40,1152]{1,0:T(8,128)(2,1)S(1)}, u32[]{:S(2)}, u32[]{:S(2)}) collective-permute-start(bf16[40,1152]{1,0:T(8,128)(2,1)S(1)} %plain_sum.3.refs_0_), channel_id=1, source_target_pairs={{0,32},{16,48},{32,64},{48,80},{64,96},{80,112},{96,0},{112,16},{1... | collective-permute-start | bytes 276488 | tf_op jit(solution)/shard_map/ppermute | solution.py:422
  132.0 11.2 %collective-permute-start.27 = (bf16[40,1152]{1,0:T(8,128)(2,1)S(1)}, bf16[40,1152]{1,0:T(8,128)(2,1)S(1)}, u32[]{:S(2)}, u32[]{:S(2)}) collective-permute-start(bf16[40,1152]{1,0:T(8,128)(2,1)S(1)} %plain_sum.3.refs_0_), channel_id=1, source_target_pairs={{0,16},{16,0},{32,48},{48,32},{64,80},{80,64},{96,112},{112,96},{1... | collective-permute-start | bytes 276488 | tf_op jit(solution)/shard_map/ppermute | solution.py:414
  138.0 5.2 %collective-permute-start.30 = (bf16[40,1152]{1,0:T(8,128)(2,1)S(1)}, bf16[40,1152]{1,0:T(8,128)(2,1)S(1)}, u32[]{:S(2)}, u32[]{:S(2)}) collective-permute-start(bf16[40,1152]{1,0:T(8,128)(2,1)S(1)} %collective-permute-done.26.refs_3_), channel_id=1, source_target_pairs={{0,16},{16,0},{32,48},{48,32},{64,80},{80,64},{96,112},{112,96},{1... | collective-permute-start | bytes 276488 | tf_op jit(solution)/shard_map/ppermute | solution.py:414
  140.5 2.7 %collective-permute-start.29 = (bf16[40,1152]{1,0:T(8,128)(2,1)S(1)}, bf16[40,1152]{1,0:T(8,128)(2,1)S(1)}, u32[]{:S(2)}, u32[]{:S(2)}) collective-permute-start(bf16[40,1152]{1,0:T(8,128)(2,1)S(1)} %collective-permute-done.25.refs_2_), channel_id=1, source_target_pairs={{0,16},{16,0},{32,48},{48,32},{64,80},{80,64},{96,112},{112,96},{1... | collective-permute-start | bytes 276488 | tf_op jit(solution)/shard_map/ppermute | solution.py:414
  142.1 2.0 %collective-permute-start.28 = (bf16[40,1152]{1,0:T(8,128)(2,1)S(1)}, bf16[40,1152]{1,0:T(8,128)(2,1)S(1)}, u32[]{:S(2)}, u32[]{:S(2)}) collective-permute-start(bf16[40,1152]{1,0:T(8,128)(2,1)S(1)} %collective-permute-done.24.refs_1_), channel_id=1, source_target_pairs={{0,16},{16,0},{32,48},{48,32},{64,80},{80,64},{96,112},{112,96},{1... | collective-permute-start | bytes 276488 | tf_op jit(solution)/shard_map/ppermute | solution.py:414
